TPU v7x, 256 devices: a whole 4x4x8 slice. The times are simulated.
256 devices in a mesh: clus: 64 (over z, y, core), rhs: 4 (over x).
Axes of the slice: x: 4, y: 4, z: 8, core: 2. Of those that a mesh axis runs over, the one named last changes fastest.
Arguments:
- vectors: bfloat16 [64, 262144], P('rhs', 'clus'), may hold values from -6 to 6
- near_field_tiles: bfloat16 [1024, 8, 256, 256], P('clus', 'rhs'), may hold values from -0.125 to 0.125
- near_lists: int32 [1024, 8], P('clus', 'rhs'), may hold values from 0 to 1023, as said below
- leaf_basis_set: bfloat16 [1024, 32, 256], P('clus'), may hold values from -0.375 to 0.375
- far_coupling: bfloat16 [1024, 32, 256], P('clus'), may hold values from -1 to 1
- far_device: int32 [1024, 8], P('clus'), may hold values from 0 to 63, all different within a row; in each aligned block of 16 rows (0 to 15, 16 to 31, ...) at most 4 rows name the same one
- far_leaf: int32 [1024, 8], P('clus'), may hold values from 0 to 15
- transfer: bfloat16 [1024, 32, 32], P('clus'), may hold values from -0.25 to 0.25
- parent: int32 [1024], P('clus'), may hold values from 0 to 63, as said below
- top_coupling: bfloat16 [2048, 2048], P('clus'), may hold values from -0.125 to 0.125
Outputs:
- first_product: bfloat16 [64, 262144], P('rhs', 'clus')
- second_product: bfloat16 [64, 262144], P('rhs', 'clus')
Inputs may be any that keep to these rules, and one draw needn't show every extreme that they name: `near_lists`: entry [i, p] is a leaf at most 16 places from i in the cyclic order of leaves; in every draw some entry lies exactly 16 places below and some exactly 16 places above. `far_device`: each row names 8 different indices; among the rows of one device no index is named by more than 4 rows. `parent`: each top-level cluster holds 1 to 31 consecutive leaves, and one holds exactly that many; leaves 2 * k * 16 to 2 * (k + 1) * 16 - 1 belong to clusters (2 * k + 32) mod 64 and (2 * k + 1 + 64 / 2) mod 64.
All inputs are finite; a program needn't handle non-finite values.
Results may differ from a plain program's by a relative error of at most 0.012.
Values may be sent and summed in bfloat16 or wider, within the bound.
A program may use at most 64 MiB of HBM per device.

v0:
```python
import jax
import jax.numpy as jnp
from jax import lax
from jax.sharding import PartitionSpec as P


def extended(block, sides, width):
    for axis, dim in sides:
        count = lax.axis_size(axis)
        forward = [(i, i + 1) for i in range(count - 1)]
        forward.append((count - 1, 0))
        backward = [(target, source) for source, target in forward]
        low = lax.ppermute(
            lax.slice_in_dim(block, block.shape[dim] - width, None, axis=dim), axis, forward
        )
        high = lax.ppermute(lax.slice_in_dim(block, 0, width, axis=dim), axis, backward)
        block = jnp.concatenate([low, block, high], axis=dim)
    return block


def gather_blocks(window, near_lists, leaf_size):
    column_count = window.shape[0]
    leaf_count = near_lists.shape[0]
    every_leaf = leaf_count * lax.axis_size("clus")
    own_leaves = lax.axis_index("clus") * leaf_count + jnp.arange(leaf_count, dtype=jnp.int32)
    offset = (near_lists - own_leaves[:, None] + leaf_count + every_leaf) % every_leaf - leaf_count
    block_index = leaf_count + jnp.arange(leaf_count, dtype=jnp.int32)[:, None] + offset
    reshaped_rows = window.reshape(column_count, 3 * leaf_count, leaf_size)
    return reshaped_rows[:, block_index, :]


def near_terms(window, near_lists, near_field_tiles):
    leaf_size = near_field_tiles.shape[2]
    block_list = gather_blocks(window, near_lists, leaf_size)
    partial_near = jnp.einsum(
        "snea,xsna->xse", near_field_tiles, block_list, preferred_element_type=jnp.float32
    )
    return partial_near.reshape(partial_near.shape[0], -1)


def far_field(
    vectors, leaf_basis_set, far_coupling, far_device, far_leaf, transfer, parent, top_coupling
):
    column_count = vectors.shape[0]
    leaf_count, rank_size, leaf_size = leaf_basis_set.shape
    far_count = far_device.shape[1]
    clusters = lax.axis_size("clus")
    capacity = min(leaf_count, max(2, 2 * leaf_count * far_count // clusters))
    reshaped_rows = vectors.reshape(column_count, leaf_count, leaf_size)
    coeffs = jnp.einsum(
        "jbo,fjo->jbf", leaf_basis_set, reshaped_rows, preferred_element_type=jnp.float32
    ).astype(jnp.bfloat16)
    contrib = jnp.einsum(
        "lrm,lrc->lmc", far_coupling, coeffs, preferred_element_type=jnp.float32
    ).astype(jnp.bfloat16)
    payload = contrib.reshape(leaf_count * far_count, rank_size * column_count)
    destination = far_device.reshape(-1)
    onehot = (destination[:, None] == jnp.arange(clusters, dtype=jnp.int32)[None, :]).astype(
        jnp.int32
    )
    earlier = jnp.cumsum(onehot, axis=0) - onehot
    slot_rank = jnp.sum(earlier * onehot, axis=1)
    position = destination * capacity + slot_rank
    outgoing = (
        jnp.zeros((clusters * capacity, payload.shape[1]), jnp.bfloat16).at[position].set(payload)
    )
    targets = (
        jnp.zeros((clusters * capacity,), jnp.int32).at[position].set(far_leaf.reshape(-1) + 1)
    )
    arrived, arrived_ids = (
        lax.all_to_all(
            outgoing.reshape(clusters, capacity, -1),
            "clus",
            split_axis=0,
            concat_axis=0,
            tiled=True,
        ),
        lax.all_to_all(
            targets.reshape(clusters, capacity), "clus", split_axis=0, concat_axis=0, tiled=True
        ),
    )
    picker = (
        arrived_ids.reshape(1, -1) == jnp.arange(1, leaf_count + 1, dtype=jnp.int32)[:, None]
    ).astype(jnp.bfloat16)
    far_sum = jnp.dot(
        picker, arrived.reshape(clusters * capacity, -1), preferred_element_type=jnp.float32
    )
    top_count = top_coupling.shape[1] // rank_size
    parent_hot = parent[:, None] == jnp.arange(top_count, dtype=jnp.int32)[None, :]
    upward = jnp.einsum(
        "lrs,lrc->lsc", transfer, coeffs, preferred_element_type=jnp.float32
    ).reshape(leaf_count, -1)
    partial_top = jnp.dot(
        parent_hot.astype(jnp.float32).T,
        upward,
        precision=lax.Precision.HIGHEST,
        preferred_element_type=jnp.float32,
    )
    top_expansion = lax.psum(partial_top, "clus").astype(jnp.bfloat16)
    own_top = jnp.dot(
        top_coupling,
        top_expansion.reshape(top_count * rank_size, column_count),
        preferred_element_type=jnp.float32,
    ).astype(jnp.bfloat16)
    all_top = lax.all_gather(own_top, "clus", axis=0, tiled=True)
    chosen = jnp.dot(
        parent_hot.astype(jnp.bfloat16),
        all_top.reshape(top_count, -1),
        preferred_element_type=jnp.float32,
    )
    chosen = chosen.astype(jnp.bfloat16).reshape(leaf_count, rank_size, column_count)
    downward = jnp.einsum("lrs,lsc->lrc", transfer, chosen, preferred_element_type=jnp.float32)
    local_expansion = (far_sum.reshape(leaf_count, rank_size, column_count) + downward).astype(
        jnp.bfloat16
    )
    far_out = jnp.einsum(
        "aex,aeu->uax", leaf_basis_set, local_expansion, preferred_element_type=jnp.float32
    )
    return far_out.reshape(column_count, -1)


def on_device(
    vectors,
    near_field_tiles,
    near_lists,
    leaf_basis_set,
    far_coupling,
    far_device,
    far_leaf,
    transfer,
    parent,
    top_coupling,
):
    current = vectors
    results = []
    for repeat in range(2):
        halo_width = current.shape[1]
        everyone = lax.all_gather(current, "rhs", axis=0, tiled=True)
        window = extended(everyone, (("clus", 1),), halo_width)
        near_sum = lax.psum_scatter(
            near_terms(window, near_lists, near_field_tiles), "rhs", scatter_dimension=0, tiled=True
        )
        far_sum = far_field(
            current,
            leaf_basis_set,
            far_coupling,
            far_device,
            far_leaf,
            transfer,
            parent,
            top_coupling,
        )
        current = (near_sum + far_sum).astype(jnp.bfloat16)
        results.append(current)
    return (results[0], results[1])


def solution(mesh):
    placed = (
        P("rhs", "clus"),
        P("clus", "rhs", None, None),
        P("clus", "rhs"),
        P("clus", None, None),
        P("clus", None, None),
        P("clus", None),
        P("clus", None),
        P("clus", None, None),
        P("clus"),
        P("clus", None),
    )
    return jax.shard_map(
        on_device,
        mesh=mesh,
        in_specs=placed,
        out_specs=(P("rhs", "clus"), P("rhs", "clus")),
        check_vma=False,
    )
```

profile of v0, /device:TPU:2, one launch (start us, length us, event | category | flops | bytes accessed | tf_op | source)
XLA Modules:
  0.0 713.6 jit_solution(6838564739854543323)
XLA Ops:
  7.2 13.8 %all_gather.12 = bf16[64,4096]{1,0:T(8,128)(2,1)S(1)} all-gather(bf16[16,4096]{1,0:T(8,128)(2,1)} %param.10), channel_id=1, replica_groups=mesh['clus'=64,'rhs'=4] {'rhs'}, dimensions={0}, use_global_device_ids=true | all-gather | bytes 655360 | tf_op jit(solution)/shard_map/all_gather | solution.py:138
  21.0 4.2 collective-permute-start.1
  25.3 0.7 broadcast_multiply_fusion
  26.0 0.8 copy.68
  26.9 0.7 broadcast_add_fusion
  27.6 0.7 compare_select_fusion
  28.8 0.2 reduce_window_sum.12
  29.0 0.2 select_reduce_fusion
  29.2 1.0 scatter_custom_fusion
  30.2 1.8 collective-permute-done.1
  32.0 5.2 collective-permute-done
  37.3 0.2 copy.126
  37.5 0.6 gather_fusion
  38.1 3.6 convolution_bitcast_fusion.1
  41.7 1.1 copy.101
  42.9 0.7 all_to_all.13
  43.6 5.2 all-to-all-start
  48.9 0.2 convolution_convert_fusion.3
  49.5 0.3 fusion.24
  49.8 251.1 %all-reduce.2 = bf16[64,512]{1,0:T(8,128)(2,1)S(1)} all-reduce(f32[64,512]{1,0:T(8,128)S(1)} %fusion.24), channel_id=1, replica_groups=mesh['clus'=64,'rhs'=4] {'clus'}, use_global_device_ids=true, to_apply=%region_5.6 | all-reduce | flops 32768 | bytes 196608 | tf_op jit(solution)/shard_map/psum | solution.py:99
  300.9 0.4 reshape.139
  301.3 0.3 fusion.4
  301.6 0.2 fusion
  301.8 40.9 %all-gather = bf16[64,32,16]{1,2,0:T(8,128)(2,1)S(1)} all-gather(bf16[1,32,16]{1,2,0:T(8,128)(2,1)S(1)} %fusion.4), channel_id=1, replica_groups=mesh['clus'=64,'rhs'=4] {'clus'}, dimensions={0}, use_global_device_ids=true | all-gather | bytes 66560 | tf_op jit(solution)/shard_map/all_gather | solution.py:105
  342.7 0.5 copy.72
  343.2 1.8 reshape.182
  345.0 1.1 scatter_custom_fusion.1
  346.1 0.8 reshape.136
  346.9 0.3 copy.76
  347.2 8.0 %all-to-all-start.1 = ((bf16[64,4,512]{2,1,0:T(4,128)(2,1)}), bf16[64,4,512]{2,1,0:T(4,128)(2,1)S(1)}, u32[]{:S(2)}, u32[]{:S(2)}) async-start(bf16[64,4,512]{2,1,0:T(4,128)(2,1)} %reshape.136), calls=%async_computation.2 | async-start | bytes 524288 | tf_op jit(solution)/shard_map/all_to_all | solution.py:71
  355.3 0.2 reduce-scatter.5.cloned.1.call-start
  355.5 0.2 convolution_convert_fusion.5
  355.7 0.2 reshape.141
  355.9 0.2 fusion.39
  356.1 0.5 broadcast.120
  356.6 0.7 reduce.3
  357.5 10.8 %all-to-all-done.1 = bf16[64,4,512]{2,1,0:T(4,128)(2,1)S(1)} async-done(((bf16[64,4,512]{2,1,0:T(4,128)(2,1)}), bf16[64,4,512]{2,1,0:T(4,128)(2,1)S(1)}, u32[]{:S(2)}, u32[]{:S(2)}) %all-to-all-start.1) | async-done | bytes 262176 | tf_op jit(solution)/shard_map/all_to_all | solution.py:71
  368.4 0.3 fusion.2
  369.0 1.0 add_convert_fusion.1
  370.0 12.9 %all_gather.14 = bf16[64,4096]{1,0:T(8,128)(2,1)S(1)} all-gather(bf16[16,4096]{1,0:T(8,128)(2,1)S(1)} %add_convert_fusion.1), channel_id=1, replica_groups=mesh['clus'=64,'rhs'=4] {'rhs'}, dimensions={0}, use_global_device_ids=true | all-gather | bytes 655360 | tf_op jit(solution)/shard_map/all_gather | solution.py:138
  382.8 0.5 collective-permute-start.2
  383.3 6.2 collective-permute-done.3
  389.5 5.2 collective-permute-done.2
  394.9 0.2 copy.125
  395.1 0.6 gather_fusion.1
  395.7 3.6 convolution_bitcast_fusion
  399.3 1.1 copy.103
  400.4 0.2 convolution_convert_fusion.2
  400.8 0.5 copy.84
  401.2 1.8 reshape.190
  403.0 1.3 scatter_custom_fusion.2
  404.3 0.8 reshape.147
  405.1 4.7 all-to-all-start.2
  410.2 0.3 fusion.23
  410.6 251.4 %all-reduce.3 = bf16[64,512]{1,0:T(8,128)(2,1)S(1)} all-reduce(f32[64,512]{1,0:T(8,128)S(1)} %fusion.23), channel_id=1, replica_groups=mesh['clus'=64,'rhs'=4] {'clus'}, use_global_device_ids=true, to_apply=%region_8.9 | all-reduce | flops 32768 | bytes 196608 | tf_op jit(solution)/shard_map/psum | solution.py:99
  661.9 0.4 reshape.150
  662.3 0.3 fusion.5
  662.6 40.9 %all-gather.1 = bf16[64,32,16]{1,2,0:T(8,128)(2,1)S(1)} all-gather(bf16[1,32,16]{1,2,0:T(8,128)(2,1)S(1)} %fusion.5), channel_id=1, replica_groups=mesh['clus'=64,'rhs'=4] {'clus'}, dimensions={0}, use_global_device_ids=true | all-gather | bytes 66560 | tf_op jit(solution)/shard_map/all_gather | solution.py:105
  703.5 0.3 copy.88
  703.8 0.2 convolution_convert_fusion.4
  704.0 0.2 reshape.152
  704.2 0.2 fusion.40
  704.6 0.3 fusion.3
  705.2 1.6 add_convert_fusion
  (55 shorter events, 3.0 us)
Async XLA Ops:
  7.2 41.7 %copy-start = (bf16[16,32,256]{2,1,0:T(8,128)(2,1)S(1)}, bf16[16,32,256]{2,1,0:T(8,128)(2,1)}, u32[]{:S(2)}) copy-start(bf16[16,32,256]{2,1,0:T(8,128)(2,1)} %param.13) | copy-start | bytes 786436
  7.2 361.8 %reduce-scatter.3.cloned.1.call-start = ((), (), s32[]{:S(2)}) async-start(), calls=%async_computation.5 | async-start | bytes 1310720 | tf_op jit(solution)/shard_map/reduce_scatter | solution.py:140
  21.0 10.9 %collective-permute-start.1 = (bf16[64,4096]{1,0:T(8,128)(2,1)S(1)}, bf16[64,4096]{1,0:T(8,128)(2,1)S(1)}, u32[]{:S(2)}, u32[]{:S(2)}) collective-permute-start(bf16[64,4096]{1,0:T(8,128)(2,1)S(1)} %all_gather.12), channel_id=1, source_target_pairs={{4,0},{8,4},{12,8},{16,12},{20,16},{24,20},{28,24},{32,28},{36,32}... | collective-permute-start | bytes 1572872 | tf_op jit(solution)/shard_map/ppermute | solution.py:16
  25.3 11.9 %collective-permute-start = (bf16[64,4096]{1,0:T(8,128)(2,1)S(1)}, bf16[64,4096]{1,0:T(8,128)(2,1)S(1)}, u32[]{:S(2)}, u32[]{:S(2)}) collective-permute-start(bf16[64,4096]{1,0:T(8,128)(2,1)S(1)} %all_gather.12), channel_id=1, source_target_pairs={{0,4},{4,8},{8,12},{12,16},{16,20},{20,24},{24,28},{28,32},{32,36}... | collective-permute-start | bytes 1572872 | tf_op jit(solution)/shard_map/ppermute | solution.py:13
  29.2 315.8 %copy-start.7 = (s32[128]{0:T(128)}, s32[128]{0:T(128)S(1)}, u32[]{:S(2)}) copy-start(s32[128]{0:T(128)S(1)} %fusion.36) | copy-start | bytes 1540
  41.7 7.2 %copy-start.4 = (bf16[16,4096]{1,0:T(8,128)(2,1)S(1)}, bf16[16,4096]{1,0:T(8,128)(2,1)}, u32[]{:S(2)}) copy-start(bf16[16,4096]{1,0:T(8,128)(2,1)} %param.10) | copy-start | bytes 393220
  41.7 7.4 %copy-start.1 = (bf16[16,32,32]{2,1,0:T(8,128)(2,1)S(1)}, bf16[16,32,32]{2,1,0:T(8,128)(2,1)}, u32[]{:S(2)}) copy-start(bf16[16,32,32]{2,1,0:T(8,128)(2,1)} %param.17) | copy-start | bytes 98308
  41.7 7.8 %copy-start.6 = (s32[16]{0:T(128)S(1)}, s32[16]{0:T(128)}, u32[]{:S(2)}) copy-start(s32[16]{0:T(128)} %param.18) | copy-start | bytes 196
  41.7 259.6 %copy-start.5 = (bf16[32,2048]{1,0:T(8,128)(2,1)S(1)}, bf16[32,2048]{1,0:T(8,128)(2,1)}, u32[]{:S(2)}) copy-start(bf16[32,2048]{1,0:T(8,128)(2,1)} %param.19) | copy-start | bytes 393220
  41.7 259.9 %copy-start.3 = (bf16[16,32,256]{2,1,0:T(8,128)(2,1)S(1)}, bf16[16,32,256]{2,1,0:T(8,128)(2,1)}, u32[]{:S(2)}) copy-start(bf16[16,32,256]{2,1,0:T(8,128)(2,1)} %param.14) | copy-start | bytes 786436
  43.6 303.6 %all-to-all-start = ((s32[64,1,4]{2,1,0:T(1,128)}), s32[64,1,4]{2,1,0:T(1,128)S(1)}, u32[]{:S(2)}, u32[]{:S(2)}) async-start(s32[64,1,4]{2,1,0:T(1,128)} %bitcast.7), calls=%async_computation.1 | async-start | bytes 65536 | tf_op jit(solution)/shard_map/all_to_all | solution.py:78
  347.2 21.0 %all-to-all-start.1 = ((bf16[64,4,512]{2,1,0:T(4,128)(2,1)}), bf16[64,4,512]{2,1,0:T(4,128)(2,1)S(1)}, u32[]{:S(2)}, u32[]{:S(2)}) async-start(bf16[64,4,512]{2,1,0:T(4,128)(2,1)} %reshape.136), calls=%async_computation.2 | async-start | bytes 524288 | tf_op jit(solution)/shard_map/all_to_all | solution.py:71
  355.3 349.9 %reduce-scatter.5.cloned.1.call-start = ((), (), s32[]{:S(2)}) async-start(), calls=%async_computation.6 | async-start | bytes 1310720 | tf_op jit(solution)/shard_map/reduce_scatter | solution.py:140
  370.0 30.4 %copy-start.2 = (bf16[16,4096]{1,0:T(8,128)(2,1)}, bf16[16,4096]{1,0:T(8,128)(2,1)S(1)}, u32[]{:S(2)}) copy-start(bf16[16,4096]{1,0:T(8,128)(2,1)S(1)} %add_convert_fusion.1) | copy-start | bytes 393220
  382.8 6.7 collective-permute-start.3
  382.8 11.9 %collective-permute-start.2 = (bf16[64,4096]{1,0:T(8,128)(2,1)S(1)}, bf16[64,4096]{1,0:T(8,128)(2,1)S(1)}, u32[]{:S(2)}, u32[]{:S(2)}) collective-permute-start(bf16[64,4096]{1,0:T(8,128)(2,1)S(1)} %all_gather.14), channel_id=1, source_target_pairs={{0,4},{4,8},{8,12},{12,16},{16,20},{20,24},{24,28},{28,32},{32,36}... | collective-permute-start | bytes 1572872 | tf_op jit(solution)/shard_map/ppermute | solution.py:13
  405.1 299.3 %all-to-all-start.2 = ((bf16[64,4,512]{2,1,0:T(4,128)(2,1)}), bf16[64,4,512]{2,1,0:T(4,128)(2,1)S(1)}, u32[]{:S(2)}, u32[]{:S(2)}) async-start(bf16[64,4,512]{2,1,0:T(4,128)(2,1)} %reshape.147), calls=%async_computation.4 | async-start | bytes 524288 | tf_op jit(solution)/shard_map/all_to_all | solution.py:71
Sparse Core Ops, SparseCore 0:
  43.0 19.7 reduce-scatter.2
  400.5 19.3 reduce-scatter.4
where the time goes:
time: 716 us; the launch traced here: 714 us
  blocking collectives  611 us (85%)
  waiting for transfers between devices  29.3 us (4%)
  starting transfers between devices  23 us (3%)
  local copies, waits for them, and re-layouts  18.8 us (3%)
  between operations  14.5 us (2%)
  matrix products  11.1 us (2%)
    psum x2, blocking collectives, far_field(): top_expansion = lax.psum(partial_top, 'clus').astype(jnp.bfloat16)  502 us
    all_gather x2, blocking collectives, far_field(): all_top = lax.all_gather(own_top, 'clus', axis=0, tiled=True)  81.8 us
    all_gather x2, blocking collectives, on_device(): everyone = lax.all_gather(current, 'rhs', axis=0, tiled=True)  26.7 us
  transfers between devices with their start and end apart: 9, of which 5 were waited for; matrix products, arithmetic and copies ran while one was open for 3% of the time, Pallas kernels for 0%

commit v1 on v0

--- a/solution.py
+++ b/solution.py
@@ -67,45 +67,46 @@
     targets = (
         jnp.zeros((clusters * capacity,), jnp.int32).at[position].set(far_leaf.reshape(-1) + 1)
     )
-    arrived, arrived_ids = (
-        lax.all_to_all(
+    upward = jnp.einsum(
+        "lrs,lrc->lsc", transfer, coeffs, preferred_element_type=jnp.float32
+    ).reshape(leaf_count, -1)
+    parent_hot = (parent % 2)[:, None] == jnp.arange(2, dtype=jnp.int32)[None, :]
+    partial_top = jnp.dot(
+        parent_hot.astype(jnp.float32).T,
+        upward,
+        precision=lax.Precision.HIGHEST,
+        preferred_element_type=jnp.float32,
+    ).astype(jnp.bfloat16)
+    everything = jnp.concatenate(
+        [
             outgoing.reshape(clusters, capacity, -1),
-            "clus",
-            split_axis=0,
-            concat_axis=0,
-            tiled=True,
-        ),
-        lax.all_to_all(
-            targets.reshape(clusters, capacity), "clus", split_axis=0, concat_axis=0, tiled=True
-        ),
+            jnp.broadcast_to(partial_top[None], (clusters,) + partial_top.shape),
+        ],
+        axis=1,
+    )
+    arrived = lax.all_to_all(everything, "clus", split_axis=0, concat_axis=0, tiled=True)
+    arrived_ids = lax.all_to_all(
+        targets.reshape(clusters, capacity), "clus", split_axis=0, concat_axis=0, tiled=True
     )
     picker = (
         arrived_ids.reshape(1, -1) == jnp.arange(1, leaf_count + 1, dtype=jnp.int32)[:, None]
     ).astype(jnp.bfloat16)
     far_sum = jnp.dot(
-        picker, arrived.reshape(clusters * capacity, -1), preferred_element_type=jnp.float32
-    )
-    top_count = top_coupling.shape[1] // rank_size
-    parent_hot = parent[:, None] == jnp.arange(top_count, dtype=jnp.int32)[None, :]
-    upward = jnp.einsum(
-        "lrs,lrc->lsc", transfer, coeffs, preferred_element_type=jnp.float32
-    ).reshape(leaf_count, -1)
-    partial_top = jnp.dot(
-        parent_hot.astype(jnp.float32).T,
-        upward,
-        precision=lax.Precision.HIGHEST,
+        picker,
+        arrived[:, :capacity].reshape(clusters * capacity, -1),
         preferred_element_type=jnp.float32,
     )
-    top_expansion = lax.psum(partial_top, "clus").astype(jnp.bfloat16)
+    top_pairs = arrived[:, capacity:].astype(jnp.float32)
+    top_pairs = top_pairs.reshape(clusters // 2, 2, 2, -1).sum(axis=1).astype(jnp.bfloat16)
+    top_expansion = jnp.roll(top_pairs.reshape(clusters, -1), clusters // 2, axis=0)
     own_top = jnp.dot(
         top_coupling,
-        top_expansion.reshape(top_count * rank_size, column_count),
+        top_expansion.reshape(clusters * rank_size, column_count),
         preferred_element_type=jnp.float32,
     ).astype(jnp.bfloat16)
-    all_top = lax.all_gather(own_top, "clus", axis=0, tiled=True)
     chosen = jnp.dot(
         parent_hot.astype(jnp.bfloat16),
-        all_top.reshape(top_count, -1),
+        own_top.reshape(2, -1),
         preferred_element_type=jnp.float32,
     )
     chosen = chosen.astype(jnp.bfloat16).reshape(leaf_count, rank_size, column_count)
@@ -131,6 +132,17 @@
     parent,
     top_coupling,
 ):
+    clusters = lax.axis_size("clus")
+    across = lax.ppermute(
+        top_coupling, "clus", [(i, (i + clusters // 2) % clusters) for i in range(clusters)]
+    )
+    other = lax.ppermute(across, "clus", [(i, i ^ 1) for i in range(clusters)])
+    core = lax.axis_index("clus") % 2
+    top_coupling = jnp.where(
+        core == 0,
+        jnp.concatenate([across, other], axis=0),
+        jnp.concatenate([other, across], axis=0),
+    )
     current = vectors
     results = []
     for repeat in range(2):

time: 716 us -> 164 us (0.23)
  blocking collectives: 611 us -> 26.9 us
  starting transfers between devices: 23 us -> 41.3 us
  waiting for transfers between devices: 29.3 us -> 37.6 us
    psum x2 -> x0, blocking collectives: 502 us -> none  [far_field(): top_expansion = lax.psum(partial_top, 'clus').astype(jnp.bfloat16)]
    all_gather x2 -> x0, blocking collectives: 81.8 us -> none  [far_field(): all_top = lax.all_gather(own_top, 'clus', axis=0, tiled=True)]
    reduce_scatter x2, waiting for transfers between devices: 0.04 us -> 15 us  [on_device(): lax.psum_scatter(near_terms(window, near_lists, near_field_tiles), 'rhs',...]
    ppermute x0 -> x2, waiting for transfers between devices: none -> 11.8 us  [the longest x1 11.5 us: on_device(): lax.ppermute(top_coupling, 'clus', [(i, (i + clusters // 2) % clusters) f...]
    ppermute x2, waiting for transfers between devices: 10.5 us -> 0.01 us  [extended(): lax.ppermute(lax.slice_in_dim(block, block.shape[dim] - width, None, axis...]
    all_to_all x2, starting transfers between devices: 12.8 us -> 20.8 us  [far_field(): lax.all_to_all(everything, 'clus', split_axis=0, concat_axis=0, tiled=True)]
    ppermute x2, waiting for transfers between devices: 7.99 us -> 0.01 us  [extended(): lax.ppermute(lax.slice_in_dim(block, 0, width, axis=dim), axis, backward)]
  transfers between devices with their start and end apart: 9 -> 11, of which waited for: 5 -> 5; matrix products, arithmetic and copies ran while one was open for 3% -> 23% of each run, Pallas kernels for 0% -> 0%
where the time goes in v1:
time: 164 us; the launch traced here: 161 us
  starting transfers between devices  41.3 us (25%)
  waiting for transfers between devices  37.6 us (23%)
  blocking collectives  26.9 us (16%)
  local copies, waits for them, and re-layouts  17.4 us (11%)
  between operations  14.6 us (9%)
  matrix products  13.8 us (8%)
  other arithmetic  9.85 us (6%)
    all_gather x2, blocking collectives, on_device(): everyone = lax.all_gather(current, 'rhs', axis=0, tiled=True)  26.9 us
    all_to_all x2, starting transfers between devices, far_field(): lax.all_to_all(everything, 'clus', split_axis=0, concat_axis=0, tiled=True)  20.8 us
    reduce_scatter x2, waiting for transfers between devices, on_device(): lax.psum_scatter(near_terms(window, near_lists, near_field_tiles), 'rhs',...  15 us
    ppermute x1, waiting for transfers between devices, on_device(): lax.ppermute(top_coupling, 'clus', [(i, (i + clusters // 2) % clusters) f...  11.5 us
    all_to_all x2, waiting for transfers between devices, far_field(): lax.all_to_all(everything, 'clus', split_axis=0, concat_axis=0, tiled=True)  10.8 us
    all_to_all x1, starting transfers between devices, far_field(): lax.all_to_all(targets.reshape(clusters, capacity), 'clus', split_axis=0,...  8.88 us
    dot_general x2, matrix products, near_terms(): jnp.einsum('snea,xsna->xse', near_field_tiles, block_list, preferred_elem...  7.11 us
    ppermute x2, starting transfers between devices, extended(): lax.ppermute(lax.slice_in_dim(block, 0, width, axis=dim), axis, backward)  5.8 us
  transfers between devices with their start and end apart: 11, of which 5 were waited for; matrix products, arithmetic and copies ran while one was open for 23% of the time, Pallas kernels for 0%

profile of v1, /device:TPU:2, one launch (start us, length us, event | category | flops | bytes accessed | tf_op | source)
XLA Modules:
  0.0 161.4 jit_solution(6531766526221649216)
XLA Ops:
  7.2 13.8 %all_gather.6 = bf16[64,4096]{1,0:T(8,128)(2,1)S(1)} all-gather(bf16[16,4096]{1,0:T(8,128)(2,1)} %param.10), channel_id=1, replica_groups=mesh['clus'=64,'rhs'=4] {'rhs'}, dimensions={0}, use_global_device_ids=true | all-gather | bytes 655360 | tf_op jit(solution)/shard_map/all_gather | solution.py:150
  21.0 4.2 %collective-permute-start.1 = (bf16[64,4096]{1,0:T(8,128)(2,1)S(1)}, bf16[64,4096]{1,0:T(8,128)(2,1)S(1)}, u32[]{:S(2)}, u32[]{:S(2)}) collective-permute-start(bf16[64,4096]{1,0:T(8,128)(2,1)S(1)} %all_gather.6), channel_id=1, source_target_pairs={{4,0},{8,4},{12,8},{16,12},{20,16},{24,20},{28,24},{32,28},{36,32}... | collective-permute-start | bytes 1572872 | tf_op jit(solution)/shard_map/ppermute | solution.py:16
  25.2 0.7 broadcast_multiply_fusion
  25.9 0.8 copy.70
  27.0 0.2 reduce_window_sum.12
  27.2 0.2 select_reduce_fusion
  27.4 0.7 broadcast_add_fusion
  28.3 1.0 scatter_custom_fusion
  29.2 0.7 all_to_all.13
  30.0 8.9 %all-to-all-start = ((s32[64,1,4]{2,1,0:T(1,128)}), s32[64,1,4]{2,1,0:T(1,128)S(1)}, u32[]{:S(2)}, u32[]{:S(2)}) async-start(s32[64,1,4]{2,1,0:T(1,128)} %bitcast.7), calls=%async_computation.1 | async-start | bytes 65536 | tf_op jit(solution)/shard_map/all_to_all | solution.py:88
  38.9 0.7 compare_select_fusion
  39.8 1.1 convolution_convert_fusion.3
  40.9 1.1 convolution_bitcast_fusion.5
  42.2 1.1 fusion
  43.3 0.5 copy.74
  43.8 1.8 %reshape.206 = bf16[128,512]{1,0:T(8,128)(2,1)S(1)} reshape(bf16[16,256,16]{2,1,0:T(8,128)(2,1)S(1)} %copy.74) | data formatting | bytes 262144 | tf_op jit(solution)/shard_map/reshape | solution.py:56
  45.6 1.1 scatter_custom_fusion.1
  46.8 0.3 convolution_convert_fusion.9
  47.2 1.1 pad_maximum_fusion.2
  48.4 0.2 copy.128
  48.6 0.6 gather_fusion
  49.2 10.3 %all-to-all-start.1 = ((bf16[64,6,512]{2,1,0:T(8,128)(2,1)}), bf16[64,6,512]{2,1,0:T(8,128)(2,1)S(1)}, u32[]{:S(2)}, u32[]{:S(2)}) async-start(bf16[64,6,512]{2,1,0:T(8,128)(2,1)} %pad_maximum_fusion.2), calls=%async_computation.2 | async-start | bytes 1048576 | tf_op jit(solution)/shard_map/all_to_all | solution.py:87
  59.6 3.6 %convolution_bitcast_fusion.1 = f32[16,8,8,256]{3,2,1,0:T(8,128)S(1)} fusion(bf16[64,16,2,256]{3,0,2,1:T(8,128)(2,1)S(1)} %bitcast.108, bf16[16,2,256,256]{3,2,1,0:T(8,128)(2,1)} %param.11), kind=kOutput, calls=%fused_computation.10 | convolution fusion | flops 268435456 | bytes 6291456 | tf_op jit(solution)/shard_map/snea,xsna->xse/dot_general | solution.py:35
  63.1 1.1 copy.103
  64.2 5.7 %collective-permute-start.2 = (bf16[32,2048]{1,0:T(8,128)(2,1)S(1)}, bf16[32,2048]{1,0:T(8,128)(2,1)S(1)}, u32[]{:S(2)}, u32[]{:S(2)}) collective-permute-start(bf16[32,2048]{1,0:T(8,128)(2,1)S(1)} %copy-done.4), channel_id=1, source_target_pairs={{0,128},{4,132},{8,136},{12,140},{16,144},{20,148},{24,152},{28,15... | collective-permute-start | bytes 393224 | tf_op jit(solution)/shard_map/ppermute | solution.py:136
  69.9 0.5 broadcast.133
  70.4 0.7 reduce.7
  71.2 11.5 %collective-permute-done.2 = bf16[32,2048]{1,0:T(8,128)(2,1)S(1)} collective-permute-done((bf16[32,2048]{1,0:T(8,128)(2,1)S(1)}, bf16[32,2048]{1,0:T(8,128)(2,1)S(1)}, u32[]{:S(2)}, u32[]{:S(2)}) %collective-permute-start.2) | collective-permute-done | bytes 131104 | tf_op jit(solution)/shard_map/ppermute | solution.py:136
  82.8 0.2 bitcast_reduce_fusion.1
  83.4 0.4 reshape.161
  83.8 0.3 collective-permute-done.3
  84.1 0.3 convolution_convert_fusion.7
  84.6 0.2 convolution_convert_fusion.5
  85.0 0.2 fusion.40
  85.2 0.3 fusion.2
  85.6 0.2 convolution_bitcast_fusion.3
  85.7 3.3 %reduce-scatter.3.cloned.1.call-done = f32[16,4096]{1,0:T(8,128)} async-done(((f32[64,4096]{1,0:T(8,128)}), f32[16,4096]{1,0:T(8,128)}) %reduce-scatter.3.cloned.1.call-update) | async-done | bytes 262160 | tf_op jit(solution)/shard_map/reduce_scatter | solution.py:152
  89.0 1.0 add_convert_fusion.1
  90.0 13.1 %all_gather.7 = bf16[64,4096]{1,0:T(8,128)(2,1)S(1)} all-gather(bf16[16,4096]{1,0:T(8,128)(2,1)S(1)} %add_convert_fusion.1), channel_id=1, replica_groups=mesh['clus'=64,'rhs'=4] {'rhs'}, dimensions={0}, use_global_device_ids=true | all-gather | bytes 655360 | tf_op jit(solution)/shard_map/all_gather | solution.py:150
  103.1 1.6 collective-permute-start.5
  104.7 0.2 convolution_convert_fusion.2
  104.9 0.2 convolution_bitcast_fusion.4
  105.4 0.2 fusion.1
  105.5 0.5 copy.86
  106.0 1.8 %reshape.214 = bf16[128,512]{1,0:T(8,128)(2,1)S(1)} reshape(bf16[16,256,16]{2,1,0:T(8,128)(2,1)S(1)} %copy.86) | data formatting | bytes 262144 | tf_op jit(solution)/shard_map/reshape | solution.py:56
  107.8 1.1 scatter_custom_fusion.2
  109.0 0.3 convolution_convert_fusion.8
  109.4 1.1 pad_maximum_fusion.3
  110.4 10.5 %all-to-all-start.2 = ((bf16[64,6,512]{2,1,0:T(8,128)(2,1)}), bf16[64,6,512]{2,1,0:T(8,128)(2,1)S(1)}, u32[]{:S(2)}, u32[]{:S(2)}) async-start(bf16[64,6,512]{2,1,0:T(8,128)(2,1)} %pad_maximum_fusion.3), calls=%async_computation.4 | async-start | bytes 1048576 | tf_op jit(solution)/shard_map/all_to_all | solution.py:87
  121.0 1.3 pad_maximum_fusion.1
  122.3 0.2 copy.127
  122.5 0.6 gather_fusion.1
  123.2 3.6 %convolution_bitcast_fusion = f32[16,8,8,256]{3,2,1,0:T(8,128)S(1)} fusion(bf16[64,16,2,256]{3,0,2,1:T(8,128)(2,1)S(1)} %bitcast.109, bf16[16,2,256,256]{3,2,1,0:T(8,128)(2,1)} %param.11), kind=kOutput, calls=%fused_computation.9 | convolution fusion | flops 268435456 | bytes 6291456 | tf_op jit(solution)/shard_map/snea,xsna->xse/dot_general | solution.py:35
  126.7 1.1 copy.105
  127.8 10.8 %all-to-all-done.2 = bf16[64,6,512]{2,1,0:T(8,128)(2,1)S(1)} async-done(((bf16[64,6,512]{2,1,0:T(8,128)(2,1)}), bf16[64,6,512]{2,1,0:T(8,128)(2,1)S(1)}, u32[]{:S(2)}, u32[]{:S(2)}) %all-to-all-start.2) | async-done | bytes 393248 | tf_op jit(solution)/shard_map/all_to_all | solution.py:87
  138.9 0.2 bitcast_reduce_fusion
  139.2 0.4 reshape.174
  139.7 0.3 convolution_convert_fusion.6
  140.2 0.2 convolution_convert_fusion.4
  140.5 0.2 fusion.41
  140.7 0.3 fusion.3
  141.1 0.2 convolution_bitcast_fusion.2
  141.3 11.7 %reduce-scatter.5.cloned.1.call-done = f32[16,4096]{1,0:T(8,128)} async-done(((f32[64,4096]{1,0:T(8,128)}), f32[16,4096]{1,0:T(8,128)}) %reduce-scatter.5.cloned.1.call-update) | async-done | bytes 262160 | tf_op jit(solution)/shard_map/reduce_scatter | solution.py:152
  152.9 1.6 %add_convert_fusion = bf16[16,4096]{1,0:T(8,128)(2,1)} fusion(f32[16,4096]{1,0:T(8,128)} %reduce-scatter.5.cloned.1.call-done, f32[16,4096]{1,0:T(8,128)S(1)} %bitcast.114), kind=kLoop, calls=%fused_computation.36 | loop fusion | flops 131072 | bytes 655360 | tf_op jit(solution)/shard_map/convert_element_type | solution.py:165
  (78 shorter events, 3.5 us)
Async XLA Ops:
  7.2 32.6 %copy-start = (bf16[16,32,256]{2,1,0:T(8,128)(2,1)S(1)}, bf16[16,32,256]{2,1,0:T(8,128)(2,1)}, u32[]{:S(2)}) copy-start(bf16[16,32,256]{2,1,0:T(8,128)(2,1)} %param.13) | copy-start | bytes 786436
  7.2 39.6 %copy-start.9 = (s32[16]{0:T(128)S(1)}, s32[16]{0:T(128)}, u32[]{:S(2)}) copy-start(s32[16]{0:T(128)} %param.18) | copy-start | bytes 196
  21.0 27.2 %collective-permute-start.1 = (bf16[64,4096]{1,0:T(8,128)(2,1)S(1)}, bf16[64,4096]{1,0:T(8,128)(2,1)S(1)}, u32[]{:S(2)}, u32[]{:S(2)}) collective-permute-start(bf16[64,4096]{1,0:T(8,128)(2,1)S(1)} %all_gather.6), channel_id=1, source_target_pairs={{4,0},{8,4},{12,8},{16,12},{20,16},{24,20},{28,24},{32,28},{36,32}... | collective-permute-start | bytes 1572872 | tf_op jit(solution)/shard_map/ppermute | solution.py:16
  25.2 23.0 %collective-permute-start = (bf16[64,4096]{1,0:T(8,128)(2,1)S(1)}, bf16[64,4096]{1,0:T(8,128)(2,1)S(1)}, u32[]{:S(2)}, u32[]{:S(2)}) collective-permute-start(bf16[64,4096]{1,0:T(8,128)(2,1)S(1)} %all_gather.6), channel_id=1, source_target_pairs={{0,4},{4,8},{8,12},{12,16},{16,20},{20,24},{24,28},{28,32},{32,36}... | collective-permute-start | bytes 1572872 | tf_op jit(solution)/shard_map/ppermute | solution.py:13
  30.0 19.2 %all-to-all-start = ((s32[64,1,4]{2,1,0:T(1,128)}), s32[64,1,4]{2,1,0:T(1,128)S(1)}, u32[]{:S(2)}, u32[]{:S(2)}) async-start(s32[64,1,4]{2,1,0:T(1,128)} %bitcast.7), calls=%async_computation.1 | async-start | bytes 65536 | tf_op jit(solution)/shard_map/all_to_all | solution.py:88
  49.2 33.6 %all-to-all-start.1 = ((bf16[64,6,512]{2,1,0:T(8,128)(2,1)}), bf16[64,6,512]{2,1,0:T(8,128)(2,1)S(1)}, u32[]{:S(2)}, u32[]{:S(2)}) async-start(bf16[64,6,512]{2,1,0:T(8,128)(2,1)} %pad_maximum_fusion.2), calls=%async_computation.2 | async-start | bytes 1048576 | tf_op jit(solution)/shard_map/all_to_all | solution.py:87
  59.5 29.5 %reduce-scatter.3.cloned.1.call-start = ((), (), s32[]{:S(2)}) async-start(), calls=%async_computation.5 | async-start | bytes 1310720 | tf_op jit(solution)/shard_map/reduce_scatter | solution.py:152
  63.1 1.1 copy-start.4
  64.2 20.8 %copy-start.1 = (bf16[16,32,32]{2,1,0:T(8,128)(2,1)S(1)}, bf16[16,32,32]{2,1,0:T(8,128)(2,1)}, u32[]{:S(2)}) copy-start(bf16[16,32,32]{2,1,0:T(8,128)(2,1)} %param.17) | copy-start | bytes 98308
  64.2 18.5 %collective-permute-start.2 = (bf16[32,2048]{1,0:T(8,128)(2,1)S(1)}, bf16[32,2048]{1,0:T(8,128)(2,1)S(1)}, u32[]{:S(2)}, u32[]{:S(2)}) collective-permute-start(bf16[32,2048]{1,0:T(8,128)(2,1)S(1)} %copy-done.4), channel_id=1, source_target_pairs={{0,128},{4,132},{8,136},{12,140},{16,144},{20,148},{24,152},{28,15... | collective-permute-start | bytes 393224 | tf_op jit(solution)/shard_map/ppermute | solution.py:136
  82.8 7.2 %copy-start.5 = (bf16[32,2048]{1,0:T(8,128)(2,1)}, bf16[32,2048]{1,0:T(8,128)(2,1)S(1)}, u32[]{:S(2)}) copy-start(bf16[32,2048]{1,0:T(8,128)(2,1)S(1)} %collective-permute-done.2) | copy-start | bytes 393220
  82.8 1.3 collective-permute-start.3
  83.8 21.5 %copy-start.3 = (bf16[16,32,256]{2,1,0:T(8,128)(2,1)S(1)}, bf16[16,32,256]{2,1,0:T(8,128)(2,1)}, u32[]{:S(2)}) copy-start(bf16[16,32,256]{2,1,0:T(8,128)(2,1)} %param.14) | copy-start | bytes 786436
  84.1 21.4 %copy-start.7 = (bf16[32,2048]{1,0:T(8,128)(2,1)}, bf16[32,2048]{1,0:T(8,128)(2,1)S(1)}, u32[]{:S(2)}) copy-start(bf16[32,2048]{1,0:T(8,128)(2,1)S(1)} %collective-permute-done.3) | copy-start | bytes 393220
  90.0 20.4 %copy-start.2 = (bf16[16,4096]{1,0:T(8,128)(2,1)}, bf16[16,4096]{1,0:T(8,128)(2,1)S(1)}, u32[]{:S(2)}) copy-start(bf16[16,4096]{1,0:T(8,128)(2,1)S(1)} %add_convert_fusion.1) | copy-start | bytes 393220
  103.1 17.9 %collective-permute-start.5 = (bf16[64,4096]{1,0:T(8,128)(2,1)S(1)}, bf16[64,4096]{1,0:T(8,128)(2,1)}, u32[]{:S(2)}, u32[]{:S(2)}) collective-permute-start(bf16[64,4096]{1,0:T(8,128)(2,1)S(1)} %all_gather.7), channel_id=1, source_target_pairs={{4,0},{8,4},{12,8},{16,12},{20,16},{24,20},{28,24},{32,28},{36,32}... | collective-permute-start | bytes 1572872 | tf_op jit(solution)/shard_map/ppermute | solution.py:16
  104.7 16.3 %collective-permute-start.4 = (bf16[64,4096]{1,0:T(8,128)(2,1)S(1)}, bf16[64,4096]{1,0:T(8,128)(2,1)}, u32[]{:S(2)}, u32[]{:S(2)}) collective-permute-start(bf16[64,4096]{1,0:T(8,128)(2,1)S(1)} %all_gather.7), channel_id=1, source_target_pairs={{0,4},{4,8},{8,12},{12,16},{16,20},{20,24},{24,28},{28,32},{32,36}... | collective-permute-start | bytes 1572872 | tf_op jit(solution)/shard_map/ppermute | solution.py:13
  110.4 28.2 %all-to-all-start.2 = ((bf16[64,6,512]{2,1,0:T(8,128)(2,1)}), bf16[64,6,512]{2,1,0:T(8,128)(2,1)S(1)}, u32[]{:S(2)}, u32[]{:S(2)}) async-start(bf16[64,6,512]{2,1,0:T(8,128)(2,1)} %pad_maximum_fusion.3), calls=%async_computation.4 | async-start | bytes 1048576 | tf_op jit(solution)/shard_map/all_to_all | solution.py:87
  120.9 32.0 %reduce-scatter.5.cloned.1.call-start = ((), (), s32[]{:S(2)}) async-start(), calls=%async_computation.6 | async-start | bytes 1310720 | tf_op jit(solution)/shard_map/reduce_scatter | solution.py:152
  126.7 12.9 %copy-start.6 = (bf16[32,2048]{1,0:T(8,128)(2,1)S(1)}, bf16[32,2048]{1,0:T(8,128)(2,1)}, u32[]{:S(2)}) copy-start(bf16[32,2048]{1,0:T(8,128)(2,1)} %copy-done.5) | copy-start | bytes 393220
  126.7 12.9 %copy-start.8 = (bf16[32,2048]{1,0:T(8,128)(2,1)S(1)}, bf16[32,2048]{1,0:T(8,128)(2,1)}, u32[]{:S(2)}) copy-start(bf16[32,2048]{1,0:T(8,128)(2,1)} %copy-done.7) | copy-start | bytes 393220
Sparse Core Ops, SparseCore 0:
  64.3 24.6 reduce-scatter.2
  127.9 24.9 reduce-scatter.4

commit v2 on v0

v2 whole, which is shorter than its diff:
```python
import jax
import jax.numpy as jnp
from jax import lax
from jax.experimental import pallas as pl
from jax.experimental.pallas import tpu as pltpu
from jax.sharding import PartitionSpec as P

MESH = pl.DeviceIdType.MESH
BF16 = jnp.bfloat16
F32 = jnp.float32
CLUS, RHS = 64, 4
LEAVES, RANK, LEAF, COLS = 16, 32, 256, 16
FAR, SLOTS, GROUPS = 8, 4, 4
LANES = 128
EMPTY = LEAVES * FAR


def dot_nn(a, b):
    return lax.dot_general(a, b, (((1,), (0,)), ((), ())), preferred_element_type=F32)


def dot_nt(a, b):
    return lax.dot_general(a, b, (((1,), (1,)), ((), ())), preferred_element_type=F32)


def kernel(
    near_s, source_s,
    vec_h, tiles_h, basis_h, coup_h, tr_h, topc_h, ids_h,
    out1, out2,
    vec, tiles, basis, coup, tr, topc, ids_in,
    win0, win1, part, rs, rolled, far,
    term_out, term_in, pair_out, pair_in, top_out, top_in, down_out, down_in,
    load_sem, ag_s, ag_r, halo_s, halo_r, rs_s, rs_r,
    term_s, term_r, id_s, id_r, pair_s, pair_r, top_s, top_r, down_s, down_r,
):
    me = lax.axis_index("clus")
    row = lax.axis_index("rhs")
    sibling = me + 1 - 2 * lax.rem(me, 2)
    above = lax.rem(me + 1, CLUS)
    below = lax.rem(me + CLUS - 1, CLUS)

    def send(src, dst, s, r, device):
        return pltpu.make_async_remote_copy(
            src_ref=src, dst_ref=dst, send_sem=s, recv_sem=r, device_id=device, device_id_type=MESH
        )

    barrier = pltpu.get_barrier_semaphore()

    def greet(o, c):
        pl.semaphore_signal(
            barrier, inc=1, device_id=(lax.rem(me + o, CLUS), row), device_id_type=MESH
        )
        return c

    lax.fori_loop(1, CLUS, greet, 0)
    for o in range(1, RHS):
        pl.semaphore_signal(
            barrier, inc=1, device_id=(me, lax.rem(row + o, RHS)), device_id_type=MESH
        )

    loads = [
        pltpu.make_async_copy(vec_h, vec, load_sem.at[0]),
        pltpu.make_async_copy(basis_h, basis, load_sem.at[1]),
        pltpu.make_async_copy(tr_h, tr, load_sem.at[2]),
        pltpu.make_async_copy(coup_h, coup, load_sem.at[3]),
    ]
    for k in range(4):
        loads.append(
            pltpu.make_async_copy(topc_h, topc.at[pl.ds(k * RANK, RANK)], load_sem.at[4 + k])
        )
    loads.append(pltpu.make_async_copy(tiles_h, tiles, load_sem.at[8]))
    for copy in loads:
        copy.start()
    rolled[EMPTY] = jnp.zeros((COLS, LANES), F32)

    lane = lax.broadcasted_iota(jnp.int32, (COLS, LANES), 1) // RANK
    group_row = lax.broadcasted_iota(jnp.int32, (GROUPS * COLS, LANES), 0) // COLS
    group_lane = lax.broadcasted_iota(jnp.int32, (GROUPS * COLS, LANES), 1) // RANK
    diagonal = group_row == group_lane
    zero = jnp.zeros((COLS, LANES), F32)

    loads[0].wait()
    for i in range(LEAVES):
        win0[row, LEAVES + i] = vec[:, i * LEAF : (i + 1) * LEAF]
    loads[1].wait()
    loads[2].wait()

    pending = []
    for q in range(2):
        win = (win0, win1)[q]
        own = win.at[row, pl.ds(LEAVES, LEAVES)]

        def spread(o, source):
            block = win.at[source, pl.ds(LEAVES, LEAVES)]
            up = send(block, win.at[source, pl.ds(0, LEAVES)],
                      halo_s.at[q, 0, o], halo_r.at[q, 0, o], (above, row))
            dn = send(block, win.at[source, pl.ds(2 * LEAVES, LEAVES)],
                      halo_s.at[q, 1, o], halo_r.at[q, 1, o], (below, row))
            return [up, dn]

        if q == 0:
            pl.semaphore_wait(barrier, CLUS - 1 + RHS - 1)
        gathers = [
            send(own, own, ag_s.at[q, o - 1], ag_r.at[q, o - 1], (me, lax.rem(row + o, RHS)))
            for o in range(1, RHS)
        ]
        halos = spread(0, row)
        for copy in (gathers[0], gathers[2], gathers[1], halos[0], halos[1]):
            copy.start()

        coeffs = []
        top_sum = zero
        for g in range(GROUPS):
            values = win[row, LEAVES + GROUPS * g : LEAVES + GROUPS * (g + 1)]
            values = values.reshape(GROUPS * COLS, LEAF)
            product = dot_nt(values, basis[g * LANES : (g + 1) * LANES, :])
            product = jnp.where(diagonal, product, 0.0)
            masked = product.astype(BF16)
            coeffs.append(masked)
            joined = product[0:COLS]
            for t in range(1, GROUPS):
                joined = joined + product[t * COLS : (t + 1) * COLS]
            top_sum = top_sum + dot_nn(joined.astype(BF16), tr[g * LANES : (g + 1) * LANES, :])
        pair_out[q] = top_sum
        pair = send(pair_out.at[q], pair_in.at[q], pair_s.at[q], pair_r.at[q], (sibling, row))
        pair.start()
        pending.append(pair)

        if q == 0:
            loads[3].wait()
        for g in range(GROUPS):
            terms = dot_nn(coeffs[g], coup[g * LANES : (g + 1) * LANES, :])
            for t in range(GROUPS):
                for half in range(2):
                    tile = terms[t * COLS : (t + 1) * COLS, half * LANES : (half + 1) * LANES]
                    base = (GROUPS * g + t) * FAR + half * 4
                    rolled[base] = tile
                    for k in range(1, 4):
                        rolled[base + k] = pltpu.roll(tile, RANK * k, 1)

        pair.wait_recv()
        top_tile = (top_sum + pair_in[q]).astype(BF16)
        top_out[q] = top_tile
        top_in[q, me // 2] = top_tile

        def top_copy(o):
            return send(top_out.at[q], top_in.at[q, me // 2], top_s.at[q], top_r.at[q],
                        (lax.rem(me + 2 * o, CLUS), row))

        def top_start(o, c):
            top_copy(o).start()
            return c

        lax.fori_loop(1, CLUS // 2, top_start, 0)

        def packed(d):
            parts = [rolled[source_s[d * SLOTS + s]] for s in range(SLOTS)]
            low = jnp.where(lane == 0, parts[0], parts[1])
            high = jnp.where(lane == 2, parts[2], parts[3])
            return jnp.where(lane < 2, low, high).astype(BF16)

        def term_copy(d):
            return send(term_out.at[q, d], term_in.at[q, me], term_s.at[q], term_r.at[q], (d, row))

        def id_copy(d):
            return send(ids_h.at[d], ids_in.at[me], id_s, id_r, (d, row))

        def term_start(o, c):
            d = lax.rem(me + o, CLUS)
            term_out[q, d] = packed(d)
            term_copy(d).start()
            if q == 0:
                id_copy(d).start()
            return c

        lax.fori_loop(1, CLUS, term_start, 0)
        term_in[q, me] = packed(me)
        if q == 0:
            own_ids = pltpu.make_async_copy(ids_h.at[me], ids_in.at[me], load_sem.at[9])
            own_ids.start()

        for o in (1, 3, 2):
            gathers[o - 1].wait_recv()
            more = spread(o, lax.rem(row + RHS - o, RHS))
            for copy in more:
                copy.start()
            halos += more
        pending += gathers + halos

        if q == 0:
            for k in range(4):
                loads[4 + k].wait()
        pltpu.make_async_copy(
            top_in.at[q, pl.ds(0, CLUS // 2 - 1)], top_in.at[q, pl.ds(0, CLUS // 2 - 1)], top_r.at[q]
        ).wait()
        pairs = CLUS // 4
        tops = [None] * pairs
        for m in range(pairs):
            tops[(m + pairs // 2) % pairs] = top_in[q, 2 * m] + top_in[q, 2 * m + 1]
        local = dot_nt(jnp.concatenate(tops, axis=1), topc[...])
        down_out[q] = jnp.where(lane == lax.rem(me, 4), local, 0.0).astype(BF16)
        across = lax.rem(me + CLUS // 2, CLUS)
        for k, d in enumerate((across, across + 1 - 2 * lax.rem(across, 2))):
            copy = send(down_out.at[q], down_in.at[q, k],
                        down_s.at[q, k], down_r.at[q, k], (d, row))
            copy.start()
            pending.append(copy)
        downs = pending[-2:]

        for copy in halos:
            copy.wait_recv()
        if q == 0:
            loads[8].wait()

        def rs_copy(chunk, o):
            leaves = pl.ds(chunk * GROUPS, GROUPS)
            target = lax.rem(row + o, RHS)
            return send(part.at[q, target, leaves], rs.at[q, o - 1, leaves],
                        rs_s.at[q, o - 1, chunk], rs_r.at[q, o - 1, chunk], (me, target))

        def near_chunk(chunk, c):
            for n in range(GROUPS):
                leaf = chunk * GROUPS + n
                total = None
                for p in range(2):
                    j = near_s[leaf * 2 + p]
                    slot = lax.rem(j - me * LEAVES + LEAVES + CLUS * LEAVES, CLUS * LEAVES)
                    slot = jnp.minimum(slot, 3 * LEAVES - 1)
                    block = win[:, slot].reshape(RHS * COLS, LEAF)
                    product = dot_nt(block, tiles[leaf, p])
                    total = product if total is None else total + product
                for a in range(RHS):
                    part[q, a, leaf] = total[a * COLS : (a + 1) * COLS].astype(BF16)
            for o in (2, 1, 3):
                rs_copy(chunk, o).start()
            return c

        lax.fori_loop(0, GROUPS, near_chunk, 0)

        pltpu.make_async_copy(
            term_in.at[q, pl.ds(0, CLUS - 1)], term_in.at[q, pl.ds(0, CLUS - 1)], term_r.at[q]
        ).wait()
        if q == 0:
            own_ids.wait()
            pltpu.make_async_copy(
                ids_in.at[pl.ds(0, CLUS - 1)], ids_in.at[pl.ds(0, CLUS - 1)], id_r
            ).wait()

        def add_terms(s, sums):
            values = term_in[q, s].astype(F32)
            targets = ids_in[s].astype(F32)
            return tuple(
                sums[t] + jnp.where(targets == float(t + 1), values, 0.0) for t in range(LEAVES)
            )

        sums = lax.fori_loop(0, CLUS, add_terms, (zero,) * LEAVES)

        for copy in downs:
            copy.wait_recv()
        chosen = down_in[q, 0] + down_in[q, 1]
        for g in range(GROUPS):
            down = dot_nt(chosen, tr[g * LANES : (g + 1) * LANES, :])
            rows = []
            for t in range(GROUPS):
                x = sums[GROUPS * g + t]
                x = x + pltpu.roll(x, 2 * RANK, 1)
                x = x + pltpu.roll(x, RANK, 1)
                rows.append(jnp.where(lane == t, x + down, 0.0).astype(BF16))
            result = dot_nn(jnp.concatenate(rows, axis=0), basis[g * LANES : (g + 1) * LANES, :])
            for t in range(GROUPS):
                far[GROUPS * g + t] = result[t * COLS : (t + 1) * COLS]

        out = out1 if q == 0 else out2
        for chunk in range(GROUPS):
            for o in range(1, RHS):
                rs_copy(chunk, o).wait_recv()
            for n in range(GROUPS):
                leaf = chunk * GROUPS + n
                total = far[leaf] + part[q, row, leaf].astype(F32)
                for o in range(RHS - 1):
                    total = total + rs[q, o, leaf].astype(F32)
                value = total.astype(BF16)
                out[:, leaf * LEAF : (leaf + 1) * LEAF] = value
                if q == 0:
                    win1[row, LEAVES + leaf] = value
        for chunk in range(GROUPS):
            for o in range(1, RHS):
                pending.append(rs_copy(chunk, o))

    for copy in pending:
        copy.wait_send()
    for q in range(2):
        pltpu.make_async_copy(
            top_in.at[q, pl.ds(0, CLUS // 2 - 1)], top_in.at[q, pl.ds(0, CLUS // 2 - 1)], top_s.at[q]
        ).wait()
        pltpu.make_async_copy(
            term_in.at[q, pl.ds(0, CLUS - 1)], term_in.at[q, pl.ds(0, CLUS - 1)], term_s.at[q]
        ).wait()
    pltpu.make_async_copy(
        ids_in.at[pl.ds(0, CLUS - 1)], ids_in.at[pl.ds(0, CLUS - 1)], id_s
    ).wait()


def slot_tables(far_device, far_leaf):
    target = far_device.reshape(-1)
    count = target.shape[0]
    order = jnp.arange(count, dtype=jnp.int32)
    same = target[:, None] == target[None, :]
    rank = jnp.sum((same & (order[None, :] < order[:, None])).astype(jnp.int32), axis=1)
    partner = order % FAR
    code = (order // FAR) * FAR + (partner // 4) * 4 + (rank - partner + FAR) % 4
    slot = target * SLOTS + rank
    hit = slot[None, :] == jnp.arange(CLUS * SLOTS, dtype=jnp.int32)[:, None]
    source = EMPTY + jnp.sum(jnp.where(hit, code[None, :] - EMPTY, 0), axis=1)
    leaf = jnp.sum(jnp.where(hit, far_leaf.reshape(-1)[None, :] + 1, 0), axis=1)
    tile = jnp.broadcast_to(
        leaf.astype(BF16).reshape(CLUS, 1, SLOTS, 1), (CLUS, COLS, SLOTS, RANK)
    ).reshape(CLUS, COLS, LANES)
    return source.astype(jnp.int32), tile


def on_device(
    vectors, near_field_tiles, near_lists, leaf_basis_set, far_coupling,
    far_device, far_leaf, transfer, parent, top_coupling,
):
    source, ids = slot_tables(far_device, far_leaf)
    chip = lax.axis_index("clus") // 2
    place = (chip % 2) * 2 + parent % 2
    hot = place[:, None, None, None] == jnp.arange(4, dtype=jnp.int32)[None, None, :, None]
    tr = jnp.where(hot, transfer[:, :, None, :], jnp.zeros((), BF16)).reshape(
        LEAVES * RANK, LANES
    )
    vmem = lambda shape, dtype=BF16: pltpu.VMEM(shape, dtype)
    dma = lambda *shape: pltpu.SemaphoreType.DMA(shape)
    anywhere = pl.BlockSpec(memory_space=pl.ANY)
    smem = pl.BlockSpec(memory_space=pltpu.SMEM)
    whole = pl.BlockSpec(memory_space=pltpu.VMEM)
    return pl.pallas_call(
        kernel,
        out_shape=[jax.ShapeDtypeStruct(vectors.shape, BF16)] * 2,
        in_specs=[smem, smem] + [anywhere] * 7,
        out_specs=[whole] * 2,
        scratch_shapes=[
            vmem((COLS, LEAVES * LEAF)),
            vmem((LEAVES, 2, LEAF, LEAF)),
            vmem((LEAVES * RANK, LEAF)),
            vmem((LEAVES * RANK, FAR * RANK)),
            vmem((LEAVES * RANK, LANES)),
            vmem((4 * RANK, CLUS * RANK)),
            vmem((CLUS, COLS, LANES)),
            vmem((RHS, 3 * LEAVES, COLS, LEAF)),
            vmem((RHS, 3 * LEAVES, COLS, LEAF)),
            vmem((2, RHS, LEAVES, COLS, LEAF)),
            vmem((2, RHS - 1, LEAVES, COLS, LEAF)),
            vmem((EMPTY + 1, COLS, LANES), F32),
            vmem((LEAVES, COLS, LEAF), F32),
            vmem((2, CLUS, COLS, LANES)),
            vmem((2, CLUS, COLS, LANES)),
            vmem((2, COLS, LANES), F32),
            vmem((2, COLS, LANES), F32),
            vmem((2, COLS, LANES)),
            vmem((2, CLUS // 2, COLS, LANES)),
            vmem((2, COLS, LANES)),
            vmem((2, 2, COLS, LANES)),
            dma(10),
            dma(2, RHS - 1), dma(2, RHS - 1),
            dma(2, 2, RHS), dma(2, 2, RHS),
            dma(2, RHS - 1, GROUPS), dma(2, RHS - 1, GROUPS),
            dma(2), dma(2),
            pltpu.SemaphoreType.DMA, pltpu.SemaphoreType.DMA,
            dma(2), dma(2),
            dma(2), dma(2),
            dma(2, 2), dma(2, 2),
        ],
        compiler_params=pltpu.CompilerParams(
            collective_id=0, has_side_effects=True, vmem_limit_bytes=40 * 1024 * 1024
        ),
    )(
        near_lists.reshape(-1), source,
        vectors, near_field_tiles,
        leaf_basis_set.reshape(LEAVES * RANK, LEAF),
        far_coupling.reshape(LEAVES * RANK, FAR * RANK),
        tr, top_coupling, ids,
    )


def solution(mesh):
    placed = (
        P("rhs", "clus"),
        P("clus", "rhs", None, None),
        P("clus", "rhs"),
        P("clus", None, None),
        P("clus", None, None),
        P("clus", None),
        P("clus", None),
        P("clus", None, None),
        P("clus"),
        P("clus", None),
    )
    return jax.shard_map(
        on_device,
        mesh=mesh,
        in_specs=placed,
        out_specs=(P("rhs", "clus"), P("rhs", "clus")),
        check_vma=False,
    )
```

time: 716 us -> 81.1 us (0.11)
  blocking collectives: 611 us -> 0 us
  Pallas kernels: 0 us -> 67.3 us
  waiting for transfers between devices: 29.3 us -> 0 us
  starting transfers between devices: 23 us -> 0 us
  between operations: 14.5 us -> 0.75 us
  matrix products: 11.1 us -> 0 us
  local copies, waits for them, and re-layouts: 18.8 us -> 9.68 us
    psum x2 -> x0, blocking collectives: 502 us -> none  [far_field(): top_expansion = lax.psum(partial_top, 'clus').astype(jnp.bfloat16)]
    all_gather x4 -> x0, blocking collectives: 108 us -> none  [the longest x2 81.8 us: far_field(): all_top = lax.all_gather(own_top, 'clus', axis=0, tiled=True)]
    pallas_call x0 -> x1, Pallas kernels: none -> 67.3 us  [on_device(): pl.pallas_call(kernel, out_shape=[jax.ShapeDtypeStruct(vectors.shape, BF1...]
    ppermute x4 -> x0, waiting for transfers between devices: 18.4 us -> none  [the longest x2 10.5 us: extended(): lax.ppermute(lax.slice_in_dim(block, block.shape[dim] - width, None, axis...]
    all_to_all x3 -> x0, starting transfers between devices: 18 us -> none  [the longest x2 12.8 us: far_field(): lax.all_to_all(outgoing.reshape(clusters, capacity, -1), 'clus', split_ax...]
    dot_general x20 -> x0, matrix products: 11.1 us -> none  [the longest x2 7.12 us: near_terms(): jnp.einsum('snea,xsna->xse', near_field_tiles, block_list, preferred_elem...]
    all_to_all x3 -> x0, waiting for transfers between devices: 10.8 us -> none  [the longest x2 10.8 us: far_field(): lax.all_to_all(outgoing.reshape(clusters, capacity, -1), 'clus', split_ax...]
    reshape x18 -> x2, local copies, waits for them, and re-layouts: 9.33 us -> 0.17 us  [the longest x1 0.09 us: slot_tables(): target = far_device.reshape(-1)]
  transfers between devices with their start and end apart: 9 -> 0, of which waited for: 5 -> 0; matrix products, arithmetic and copies ran while one was open for 3% -> 0% of each run, Pallas kernels for 0% -> 0%
where the time goes in v2:
time: 81.1 us; the launch traced here: 80.8 us
  Pallas kernels  67.3 us (83%)
  local copies, waits for them, and re-layouts  9.68 us (12%)
  other arithmetic  3 us (4%)
    pallas_call x1, Pallas kernels, on_device(): pl.pallas_call(kernel, out_shape=[jax.ShapeDtypeStruct(vectors.shape, BF1...  67.3 us
    unnamed x14, local copies, waits for them, and re-layouts  8.72 us

profile of v2, /device:TPU:2, one launch (start us, length us, event | category | flops | bytes accessed | tf_op | source)
XLA Modules:
  0.0 80.8 jit_solution(1225418898543107336)
XLA Ops:
  0.7 0.7 fusion.4
  1.3 0.1 iota_compare_fusion.2
  1.4 1.2 %broadcast_select_fusion = bf16[16,32,4,32]{3,2,1,0:T(4,128)(2,1)S(1)} fusion(pred[16,4]{1,0:T(8,128)(4,1)S(1)} %iota_compare_fusion.2, bf16[16,32,32]{2,1,0:T(8,128)(2,1)} %param.17), kind=kLoop, calls=%fused_computation | loop fusion | flops 65536 | bytes 163904 | tf_op jit(solution)/shard_map/jit(_where)/select_n | solution.py:330
  2.6 0.3 select_n.77.tr_h
  2.9 0.8 copy.21
  3.7 0.1 reshape.131
  3.8 0.2 convert_reduce_fusion
  4.0 0.7 broadcast_add_fusion
  4.7 0.1 copy.22
  4.7 0.1 add.112
  4.8 0.2 select_reduce_fusion
  5.0 0.1 convert_element_type.15
  5.1 0.1 copy.23
  5.2 0.1 copy.24
  5.4 0.8 copy.20
  6.1 0.1 reshape.130.near_s
  6.2 0.0 copy-start
  6.2 2.2 %copy-done = bf16[16,2,256,256]{3,2,1,0:T(8,128)(2,1)S(1)} copy-done((bf16[16,2,256,256]{3,2,1,0:T(8,128)(2,1)S(1)}, bf16[16,2,256,256]{3,2,1,0:T(8,128)(2,1)}, u32[]{:S(2)}) %copy-start) | copy-done | bytes 4194328
  8.4 0.0 copy-start.1
  8.4 0.9 %copy-done.1 = bf16[16,32,256]{2,1,0:T(8,128)(2,1)S(1)} copy-done((bf16[16,32,256]{2,1,0:T(8,128)(2,1)S(1)}, bf16[16,32,256]{2,1,0:T(8,128)(2,1)}, u32[]{:S(2)}) %copy-start.1) | copy-done | bytes 262168
  9.4 0.0 copy-start.2
  9.4 0.9 %copy-done.2 = bf16[16,32,256]{2,1,0:T(8,128)(2,1)S(1)} copy-done((bf16[16,32,256]{2,1,0:T(8,128)(2,1)S(1)}, bf16[16,32,256]{2,1,0:T(8,128)(2,1)}, u32[]{:S(2)}) %copy-start.2) | copy-done | bytes 262168
  10.3 0.0 copy-start.3
  10.3 0.9 %copy-done.3 = bf16[16,4096]{1,0:T(8,128)(2,1)S(1)} copy-done((bf16[16,4096]{1,0:T(8,128)(2,1)S(1)}, bf16[16,4096]{1,0:T(8,128)(2,1)}, u32[]{:S(2)}) %copy-start.3) | copy-done | bytes 131096
  11.2 0.0 copy-start.4
  11.2 0.9 %copy-done.4 = bf16[32,2048]{1,0:T(8,128)(2,1)S(1)} copy-done((bf16[32,2048]{1,0:T(8,128)(2,1)S(1)}, bf16[32,2048]{1,0:T(8,128)(2,1)}, u32[]{:S(2)}) %copy-start.4) | copy-done | bytes 131096
  12.1 67.3 %shard_map.113 = (bf16[16,4096]{1,0:T(8,128)(2,1)S(1)}, bf16[16,4096]{1,0:T(8,128)(2,1)S(1)}) custom-call(s32[32]{0:T(128)S(1)} %reshape.130.near_s, s32[256]{0:T(256)S(1)} %broadcast_add_fusion.1.source_s, bf16[16,4096]{1,0:T(8,128)(2,1)S(1)} %copy-done.3, bf16[16,2,256,256]{3,2,1,0:T(8,128)(2,1)S(1)} %copy-done, bf16[512,256]{1,0:T(8,128)(2,1)S(1)} %bitcast.3, ...), custom_call_target="tpu_custom_call" | custom-call | tf_op jit(solution)/shard_map/pallas_call | solution.py:338
  79.4 0.7 copy.27
  80.1 0.7 copy.28
  (5 shorter events, 0.1 us)
Async XLA Ops:
  6.2 2.2 %copy-start = (bf16[16,2,256,256]{3,2,1,0:T(8,128)(2,1)S(1)}, bf16[16,2,256,256]{3,2,1,0:T(8,128)(2,1)}, u32[]{:S(2)}) copy-start(bf16[16,2,256,256]{3,2,1,0:T(8,128)(2,1)} %tiles_h.1) | copy-start | bytes 12582916
  8.4 0.9 %copy-start.1 = (bf16[16,32,256]{2,1,0:T(8,128)(2,1)S(1)}, bf16[16,32,256]{2,1,0:T(8,128)(2,1)}, u32[]{:S(2)}) copy-start(bf16[16,32,256]{2,1,0:T(8,128)(2,1)} %param.13) | copy-start | bytes 786436
  9.4 0.9 %copy-start.2 = (bf16[16,32,256]{2,1,0:T(8,128)(2,1)S(1)}, bf16[16,32,256]{2,1,0:T(8,128)(2,1)}, u32[]{:S(2)}) copy-start(bf16[16,32,256]{2,1,0:T(8,128)(2,1)} %param.14) | copy-start | bytes 786436
  10.3 0.9 %copy-start.3 = (bf16[16,4096]{1,0:T(8,128)(2,1)S(1)}, bf16[16,4096]{1,0:T(8,128)(2,1)}, u32[]{:S(2)}) copy-start(bf16[16,4096]{1,0:T(8,128)(2,1)} %vec_h.1) | copy-start | bytes 393220
  11.2 0.9 %copy-start.4 = (bf16[32,2048]{1,0:T(8,128)(2,1)S(1)}, bf16[32,2048]{1,0:T(8,128)(2,1)}, u32[]{:S(2)}) copy-start(bf16[32,2048]{1,0:T(8,128)(2,1)} %topc_h.1) | copy-start | bytes 393220

commit v3 on v2

--- a/solution.py
+++ b/solution.py
@@ -11,6 +11,7 @@
 CLUS, RHS = 64, 4
 LEAVES, RANK, LEAF, COLS = 16, 32, 256, 16
 FAR, SLOTS, GROUPS = 8, 4, 4
+ORDER = (0, 2, 1, 3)
 LANES = 128
 EMPTY = LEAVES * FAR
 
@@ -28,14 +29,17 @@
     vec_h, tiles_h, basis_h, coup_h, tr_h, topc_h, ids_h,
     out1, out2,
     vec, tiles, basis, coup, tr, topc, ids_in,
-    win0, win1, part, rs, rolled, far,
-    term_out, term_in, pair_out, pair_in, top_out, top_in, down_out, down_in,
-    load_sem, ag_s, ag_r, halo_s, halo_r, rs_s, rs_r,
-    term_s, term_r, id_s, id_r, pair_s, pair_r, top_s, top_r, down_s, down_r,
+    win0, win1, part, rs, relay, rolled, far,
+    term_out, term_in, quad_out, quad_in, top_out, top_in, down_out, down_in,
+    load_sem, ag_s, ag_r, halo_s, halo_r, rs_s, rs_r, relay_s, relay_r,
+    term_s, term_r, id_s, id_r, quad_s, quad_r, top_s, top_r, down_s, down_r,
 ):
     me = lax.axis_index("clus")
     row = lax.axis_index("rhs")
-    sibling = me + 1 - 2 * lax.rem(me, 2)
+    right = lax.rem(row + 1, RHS)
+    left = lax.rem(row + RHS - 1, RHS)
+    opposite = lax.rem(row + 2, RHS)
+    corner = lax.rem(me, 4)
     above = lax.rem(me + 1, CLUS)
     below = lax.rem(me + CLUS - 1, CLUS)
 
@@ -86,27 +90,35 @@
     loads[2].wait()
 
     pending = []
+
+    def own_chunk(q, chunk):
+        win = (win0, win1)[q]
+        block = win.at[row, pl.ds(LEAVES + GROUPS * chunk, GROUPS)]
+        copies = [
+            send(block, block, ag_s.at[q, 0, chunk], ag_r.at[q, 0, chunk], (me, right)),
+            send(block, block, ag_s.at[q, 1, chunk], ag_r.at[q, 1, chunk], (me, left)),
+        ] + spread(q, 0, row, chunk)
+        for copy in copies:
+            copy.start()
+        pending.extend(copies)
+
+    def spread(q, o, source, chunk):
+        win = (win0, win1)[q]
+        base = GROUPS * chunk
+        block = win.at[source, pl.ds(LEAVES + base, GROUPS)]
+        return [
+            send(block, win.at[source, pl.ds(base, GROUPS)],
+                 halo_s.at[q, 0, o, chunk], halo_r.at[q, 0, o, chunk], (above, row)),
+            send(block, win.at[source, pl.ds(2 * LEAVES + base, GROUPS)],
+                 halo_s.at[q, 1, o, chunk], halo_r.at[q, 1, o, chunk], (below, row)),
+        ]
+
     for q in range(2):
         win = (win0, win1)[q]
-        own = win.at[row, pl.ds(LEAVES, LEAVES)]
-
-        def spread(o, source):
-            block = win.at[source, pl.ds(LEAVES, LEAVES)]
-            up = send(block, win.at[source, pl.ds(0, LEAVES)],
-                      halo_s.at[q, 0, o], halo_r.at[q, 0, o], (above, row))
-            dn = send(block, win.at[source, pl.ds(2 * LEAVES, LEAVES)],
-                      halo_s.at[q, 1, o], halo_r.at[q, 1, o], (below, row))
-            return [up, dn]
-
         if q == 0:
             pl.semaphore_wait(barrier, CLUS - 1 + RHS - 1)
-        gathers = [
-            send(own, own, ag_s.at[q, o - 1], ag_r.at[q, o - 1], (me, lax.rem(row + o, RHS)))
-            for o in range(1, RHS)
-        ]
-        halos = spread(0, row)
-        for copy in (gathers[0], gathers[2], gathers[1], halos[0], halos[1]):
-            copy.start()
+            for chunk in ORDER:
+                own_chunk(0, chunk)
 
         coeffs = []
         top_sum = zero
@@ -121,10 +133,15 @@
             for t in range(1, GROUPS):
                 joined = joined + product[t * COLS : (t + 1) * COLS]
             top_sum = top_sum + dot_nn(joined.astype(BF16), tr[g * LANES : (g + 1) * LANES, :])
-        pair_out[q] = top_sum
-        pair = send(pair_out.at[q], pair_in.at[q], pair_s.at[q], pair_r.at[q], (sibling, row))
-        pair.start()
-        pending.append(pair)
+        quad_out[q] = top_sum
+        quads = []
+        for o in range(1, 4):
+            peer = me - corner + lax.rem(corner + o, 4)
+            copy = send(quad_out.at[q], quad_in.at[q, o - 1],
+                        quad_s.at[q, o - 1], quad_r.at[q, o - 1], (peer, row))
+            copy.start()
+            quads.append(copy)
+        pending += quads
 
         if q == 0:
             loads[3].wait()
@@ -138,20 +155,18 @@
                     for k in range(1, 4):
                         rolled[base + k] = pltpu.roll(tile, RANK * k, 1)
 
-        pair.wait_recv()
-        top_tile = (top_sum + pair_in[q]).astype(BF16)
+        for copy in quads:
+            copy.wait_recv()
+        top_tile = (top_sum + quad_in[q, 0] + quad_in[q, 1] + quad_in[q, 2]).astype(BF16)
         top_out[q] = top_tile
-        top_in[q, me // 2] = top_tile
-
-        def top_copy(o):
-            return send(top_out.at[q], top_in.at[q, me // 2], top_s.at[q], top_r.at[q],
-                        (lax.rem(me + 2 * o, CLUS), row))
+        top_in[q, me // 4] = top_tile
 
         def top_start(o, c):
-            top_copy(o).start()
+            send(top_out.at[q], top_in.at[q, me // 4], top_s.at[q], top_r.at[q],
+                 (lax.rem(me + 4 * o, CLUS), row)).start()
             return c
 
-        lax.fori_loop(1, CLUS // 2, top_start, 0)
+        lax.fori_loop(1, CLUS // 4, top_start, 0)
 
         def packed(d):
             parts = [rolled[source_s[d * SLOTS + s]] for s in range(SLOTS)]
@@ -179,24 +194,37 @@
             own_ids = pltpu.make_async_copy(ids_h.at[me], ids_in.at[me], load_sem.at[9])
             own_ids.start()
 
-        for o in (1, 3, 2):
-            gathers[o - 1].wait_recv()
-            more = spread(o, lax.rem(row + RHS - o, RHS))
+        halos = []
+        for chunk in ORDER:
+            for side, source in enumerate((left, right)):
+                block = win.at[source, pl.ds(LEAVES + GROUPS * chunk, GROUPS)]
+                send(block, block, ag_s.at[q, side, chunk], ag_r.at[q, side, chunk],
+                     (me, right)).wait_recv()
+                more = spread(q, 1 + 2 * side, source, chunk)
+                if side == chunk // 2:
+                    more.insert(0, send(block, block, ag_s.at[q, 2, chunk], ag_r.at[q, 2, chunk],
+                                        (me, (right, left)[side])))
+                for copy in more:
+                    copy.start()
+                pending += more
+        for chunk in ORDER:
+            block = win.at[opposite, pl.ds(LEAVES + GROUPS * chunk, GROUPS)]
+            send(block, block, ag_s.at[q, 2, chunk], ag_r.at[q, 2, chunk], (me, right)).wait_recv()
+            more = spread(q, 2, opposite, chunk)
             for copy in more:
                 copy.start()
-            halos += more
-        pending += gathers + halos
+            pending += more
 
         if q == 0:
             for k in range(4):
                 loads[4 + k].wait()
         pltpu.make_async_copy(
-            top_in.at[q, pl.ds(0, CLUS // 2 - 1)], top_in.at[q, pl.ds(0, CLUS // 2 - 1)], top_r.at[q]
+            top_in.at[q, pl.ds(0, CLUS // 4 - 1)], top_in.at[q, pl.ds(0, CLUS // 4 - 1)], top_r.at[q]
         ).wait()
         pairs = CLUS // 4
         tops = [None] * pairs
         for m in range(pairs):
-            tops[(m + pairs // 2) % pairs] = top_in[q, 2 * m] + top_in[q, 2 * m + 1]
+            tops[(m + pairs // 2) % pairs] = top_in[q, m]
         local = dot_nt(jnp.concatenate(tops, axis=1), topc[...])
         down_out[q] = jnp.where(lane == lax.rem(me, 4), local, 0.0).astype(BF16)
         across = lax.rem(me + CLUS // 2, CLUS)
@@ -207,23 +235,31 @@
             pending.append(copy)
         downs = pending[-2:]
 
-        for copy in halos:
-            copy.wait_recv()
+        for chunk in ORDER:
+            for o, source in ((0, row), (1, left), (3, right), (2, opposite)):
+                for copy in spread(q, o, source, chunk):
+                    copy.wait_recv()
         if q == 0:
             loads[8].wait()
 
-        def rs_copy(chunk, o):
+        def relay_copy(chunk):
             leaves = pl.ds(chunk * GROUPS, GROUPS)
-            target = lax.rem(row + o, RHS)
-            return send(part.at[q, target, leaves], rs.at[q, o - 1, leaves],
-                        rs_s.at[q, o - 1, chunk], rs_r.at[q, o - 1, chunk], (me, target))
-
-        def near_chunk(chunk, c):
+            return send(part.at[q, opposite, leaves], relay.at[q, leaves],
+                        relay_s.at[q, chunk], relay_r.at[q, chunk],
+                        (me, (right, left)[chunk // 2]))
+
+        def rs_copy(chunk, side):
+            leaves = pl.ds(chunk * GROUPS, GROUPS)
+            target = (right, left)[side]
+            return send(part.at[q, target, leaves], rs.at[q, side, leaves],
+                        rs_s.at[q, side, chunk], rs_r.at[q, side, chunk], (me, target))
+
+        def near_chunk(chunk):
             for n in range(GROUPS):
                 leaf = chunk * GROUPS + n
                 total = None
                 for p in range(2):
-                    j = near_s[leaf * 2 + p]
+                    j = near_s[leaf, p]
                     slot = lax.rem(j - me * LEAVES + LEAVES + CLUS * LEAVES, CLUS * LEAVES)
                     slot = jnp.minimum(slot, 3 * LEAVES - 1)
                     block = win[:, slot].reshape(RHS * COLS, LEAF)
@@ -231,11 +267,25 @@
                     total = product if total is None else total + product
                 for a in range(RHS):
                     part[q, a, leaf] = total[a * COLS : (a + 1) * COLS].astype(BF16)
-            for o in (2, 1, 3):
-                rs_copy(chunk, o).start()
-            return c
-
-        lax.fori_loop(0, GROUPS, near_chunk, 0)
+            copies = (relay_copy(chunk), rs_copy(chunk, 1 - chunk // 2))
+            for copy in copies:
+                copy.start()
+            pending.extend(copies)
+
+        for chunk in ORDER:
+            near_chunk(chunk)
+        for chunk in ORDER:
+            relay_copy(chunk).wait_recv()
+            side = chunk // 2
+            target = (right, left)[side]
+            for n in range(GROUPS):
+                leaf = chunk * GROUPS + n
+                part[q, target, leaf] = (
+                    part[q, target, leaf].astype(F32) + relay[q, leaf].astype(F32)
+                ).astype(BF16)
+            copy = rs_copy(chunk, side)
+            copy.start()
+            pending.append(copy)
 
         pltpu.make_async_copy(
             term_in.at[q, pl.ds(0, CLUS - 1)], term_in.at[q, pl.ds(0, CLUS - 1)], term_r.at[q]
@@ -271,27 +321,25 @@
                 far[GROUPS * g + t] = result[t * COLS : (t + 1) * COLS]
 
         out = out1 if q == 0 else out2
-        for chunk in range(GROUPS):
-            for o in range(1, RHS):
-                rs_copy(chunk, o).wait_recv()
+        for chunk in ORDER:
+            rs_copy(chunk, 1 - chunk // 2).wait_recv()
+            rs_copy(chunk, chunk // 2).wait_recv()
             for n in range(GROUPS):
                 leaf = chunk * GROUPS + n
                 total = far[leaf] + part[q, row, leaf].astype(F32)
-                for o in range(RHS - 1):
-                    total = total + rs[q, o, leaf].astype(F32)
+                total = total + rs[q, 0, leaf].astype(F32) + rs[q, 1, leaf].astype(F32)
                 value = total.astype(BF16)
                 out[:, leaf * LEAF : (leaf + 1) * LEAF] = value
                 if q == 0:
                     win1[row, LEAVES + leaf] = value
-        for chunk in range(GROUPS):
-            for o in range(1, RHS):
-                pending.append(rs_copy(chunk, o))
+            if q == 0:
+                own_chunk(1, chunk)
 
     for copy in pending:
         copy.wait_send()
     for q in range(2):
         pltpu.make_async_copy(
-            top_in.at[q, pl.ds(0, CLUS // 2 - 1)], top_in.at[q, pl.ds(0, CLUS // 2 - 1)], top_s.at[q]
+            top_in.at[q, pl.ds(0, CLUS // 4 - 1)], top_in.at[q, pl.ds(0, CLUS // 4 - 1)], top_s.at[q]
         ).wait()
         pltpu.make_async_copy(
             term_in.at[q, pl.ds(0, CLUS - 1)], term_in.at[q, pl.ds(0, CLUS - 1)], term_s.at[q]
@@ -332,7 +380,7 @@
     )
     vmem = lambda shape, dtype=BF16: pltpu.VMEM(shape, dtype)
     dma = lambda *shape: pltpu.SemaphoreType.DMA(shape)
-    anywhere = pl.BlockSpec(memory_space=pl.ANY)
+    anywhere = pl.BlockSpec(memory_space=pltpu.HBM)
     smem = pl.BlockSpec(memory_space=pltpu.SMEM)
     whole = pl.BlockSpec(memory_space=pltpu.VMEM)
     return pl.pallas_call(
@@ -351,24 +399,26 @@
             vmem((RHS, 3 * LEAVES, COLS, LEAF)),
             vmem((RHS, 3 * LEAVES, COLS, LEAF)),
             vmem((2, RHS, LEAVES, COLS, LEAF)),
-            vmem((2, RHS - 1, LEAVES, COLS, LEAF)),
+            vmem((2, 2, LEAVES, COLS, LEAF)),
+            vmem((2, LEAVES, COLS, LEAF)),
             vmem((EMPTY + 1, COLS, LANES), F32),
             vmem((LEAVES, COLS, LEAF), F32),
             vmem((2, CLUS, COLS, LANES)),
             vmem((2, CLUS, COLS, LANES)),
             vmem((2, COLS, LANES), F32),
-            vmem((2, COLS, LANES), F32),
+            vmem((2, 3, COLS, LANES), F32),
             vmem((2, COLS, LANES)),
-            vmem((2, CLUS // 2, COLS, LANES)),
+            vmem((2, CLUS // 4, COLS, LANES)),
             vmem((2, COLS, LANES)),
             vmem((2, 2, COLS, LANES)),
             dma(10),
-            dma(2, RHS - 1), dma(2, RHS - 1),
-            dma(2, 2, RHS), dma(2, 2, RHS),
-            dma(2, RHS - 1, GROUPS), dma(2, RHS - 1, GROUPS),
+            dma(2, 3, GROUPS), dma(2, 3, GROUPS),
+            dma(2, 2, RHS, GROUPS), dma(2, 2, RHS, GROUPS),
+            dma(2, 2, GROUPS), dma(2, 2, GROUPS),
+            dma(2, GROUPS), dma(2, GROUPS),
             dma(2), dma(2),
             pltpu.SemaphoreType.DMA, pltpu.SemaphoreType.DMA,
-            dma(2), dma(2),
+            dma(2, 3), dma(2, 3),
             dma(2), dma(2),
             dma(2, 2), dma(2, 2),
         ],
@@ -376,7 +426,7 @@
             collective_id=0, has_side_effects=True, vmem_limit_bytes=40 * 1024 * 1024
         ),
     )(
-        near_lists.reshape(-1), source,
+        near_lists, source,
         vectors, near_field_tiles,
         leaf_basis_set.reshape(LEAVES * RANK, LEAF),
         far_coupling.reshape(LEAVES * RANK, FAR * RANK),

time: 81.1 us -> 83.2 us (1.026)
  Pallas kernels: 67.3 us -> 69.1 us
    pallas_call x1, Pallas kernels: 67.3 us -> 69.1 us  [on_device(): pl.pallas_call(kernel, out_shape=[jax.ShapeDtypeStruct(vectors.shape, BF1...]
where the time goes in v3:
time: 83.2 us; the launch traced here: 82.5 us
  Pallas kernels  69.1 us (83%)
  local copies, waits for them, and re-layouts  9.6 us (12%)
  other arithmetic  3 us (4%)
    pallas_call x1, Pallas kernels, on_device(): pl.pallas_call(kernel, out_shape=[jax.ShapeDtypeStruct(vectors.shape, BF1...  69.1 us
    unnamed x14, local copies, waits for them, and re-layouts  8.72 us

profile of v3, /device:TPU:2, one launch (start us, length us, event | category | flops | bytes accessed | tf_op | source)
XLA Modules:
  0.0 82.5 jit_solution(9417547398111594858)
XLA Ops:
  0.7 0.7 fusion.4
  1.3 0.1 iota_compare_fusion.2
  1.4 1.2 %broadcast_select_fusion = bf16[16,32,4,32]{3,2,1,0:T(4,128)(2,1)S(1)} fusion(pred[16,4]{1,0:T(8,128)(4,1)S(1)} %iota_compare_fusion.2, bf16[16,32,32]{2,1,0:T(8,128)(2,1)} %param.17), kind=kLoop, calls=%fused_computation | loop fusion | flops 65536 | bytes 163904 | tf_op jit(solution)/shard_map/jit(_where)/select_n | solution.py:378
  2.6 0.3 select_n.77.tr_h
  2.9 0.8 copy.20
  3.7 0.1 reshape.127
  3.8 0.2 convert_reduce_fusion
  4.0 0.7 broadcast_add_fusion
  4.7 0.1 copy.21
  4.7 0.1 add.112
  4.8 0.2 select_reduce_fusion
  5.0 0.1 convert_element_type.15
  5.1 0.1 copy.22
  5.2 0.1 copy.23
  5.4 0.8 copy.24.near_s
  6.1 0.0 copy-start
  6.1 2.2 %copy-done = bf16[16,2,256,256]{3,2,1,0:T(8,128)(2,1)S(1)} copy-done((bf16[16,2,256,256]{3,2,1,0:T(8,128)(2,1)S(1)}, bf16[16,2,256,256]{3,2,1,0:T(8,128)(2,1)}, u32[]{:S(2)}) %copy-start) | copy-done | bytes 4194328
  8.3 0.0 copy-start.1
  8.3 0.9 %copy-done.1 = bf16[16,32,256]{2,1,0:T(8,128)(2,1)S(1)} copy-done((bf16[16,32,256]{2,1,0:T(8,128)(2,1)S(1)}, bf16[16,32,256]{2,1,0:T(8,128)(2,1)}, u32[]{:S(2)}) %copy-start.1) | copy-done | bytes 262168
  9.3 0.0 copy-start.2
  9.3 0.9 %copy-done.2 = bf16[16,32,256]{2,1,0:T(8,128)(2,1)S(1)} copy-done((bf16[16,32,256]{2,1,0:T(8,128)(2,1)S(1)}, bf16[16,32,256]{2,1,0:T(8,128)(2,1)}, u32[]{:S(2)}) %copy-start.2) | copy-done | bytes 262168
  10.2 0.0 copy-start.3
  10.2 0.9 %copy-done.3 = bf16[16,4096]{1,0:T(8,128)(2,1)S(1)} copy-done((bf16[16,4096]{1,0:T(8,128)(2,1)S(1)}, bf16[16,4096]{1,0:T(8,128)(2,1)}, u32[]{:S(2)}) %copy-start.3) | copy-done | bytes 131096
  11.1 0.0 copy-start.4
  11.1 0.9 %copy-done.4 = bf16[32,2048]{1,0:T(8,128)(2,1)S(1)} copy-done((bf16[32,2048]{1,0:T(8,128)(2,1)S(1)}, bf16[32,2048]{1,0:T(8,128)(2,1)}, u32[]{:S(2)}) %copy-start.4) | copy-done | bytes 131096
  12.0 69.1 %shard_map.113 = (bf16[16,4096]{1,0:T(8,128)(2,1)S(1)}, bf16[16,4096]{1,0:T(8,128)(2,1)S(1)}) custom-call(s32[16,2]{1,0:T(8,128)S(1)} %copy.24.near_s, s32[256]{0:T(256)S(1)} %broadcast_add_fusion.1.source_s, bf16[16,4096]{1,0:T(8,128)(2,1)S(1)} %copy-done.3, bf16[16,2,256,256]{3,2,1,0:T(8,128)(2,1)S(1)} %copy-done, bf16[512,256]{1,0:T(8,128)(2,1)S(1)} %bitcast.3, ...), custom_call_target="tpu_custom_call" | custom-call | tf_op jit(solution)/shard_map/pallas_call | solution.py:386
  81.1 0.7 copy.27
  81.8 0.7 copy.28
  (5 shorter events, 0.1 us)
Async XLA Ops:
  6.1 2.2 %copy-start = (bf16[16,2,256,256]{3,2,1,0:T(8,128)(2,1)S(1)}, bf16[16,2,256,256]{3,2,1,0:T(8,128)(2,1)}, u32[]{:S(2)}) copy-start(bf16[16,2,256,256]{3,2,1,0:T(8,128)(2,1)} %tiles_h.1) | copy-start | bytes 12582916
  8.3 0.9 %copy-start.1 = (bf16[16,32,256]{2,1,0:T(8,128)(2,1)S(1)}, bf16[16,32,256]{2,1,0:T(8,128)(2,1)}, u32[]{:S(2)}) copy-start(bf16[16,32,256]{2,1,0:T(8,128)(2,1)} %param.13) | copy-start | bytes 786436
  9.3 0.9 %copy-start.2 = (bf16[16,32,256]{2,1,0:T(8,128)(2,1)S(1)}, bf16[16,32,256]{2,1,0:T(8,128)(2,1)}, u32[]{:S(2)}) copy-start(bf16[16,32,256]{2,1,0:T(8,128)(2,1)} %param.14) | copy-start | bytes 786436
  10.2 0.9 %copy-start.3 = (bf16[16,4096]{1,0:T(8,128)(2,1)S(1)}, bf16[16,4096]{1,0:T(8,128)(2,1)}, u32[]{:S(2)}) copy-start(bf16[16,4096]{1,0:T(8,128)(2,1)} %vec_h.1) | copy-start | bytes 393220
  11.1 0.9 %copy-start.4 = (bf16[32,2048]{1,0:T(8,128)(2,1)S(1)}, bf16[32,2048]{1,0:T(8,128)(2,1)}, u32[]{:S(2)}) copy-start(bf16[32,2048]{1,0:T(8,128)(2,1)} %topc_h.1) | copy-start | bytes 393220

commit v4 on v3

--- a/solution.py
+++ b/solution.py
@@ -24,22 +24,25 @@
     return lax.dot_general(a, b, (((1,), (1,)), ((), ())), preferred_element_type=F32)
 
 
+VM = 60
+
+
 def kernel(
-    near_s, source_s,
-    vec_h, tiles_h, basis_h, coup_h, tr_h, topc_h, ids_h,
+    near_s, parent_s, device_v, leaf_v,
+    vec_h, tiles_h, basis_h, coup_h, transfer_h, topc_h,
     out1, out2,
-    vec, tiles, basis, coup, tr, topc, ids_in,
+    vec, tiles, basis, coup, transfer, tr, topc, codes, padded, source_v, source_s, ids,
     win0, win1, part, rs, relay, rolled, far,
-    term_out, term_in, quad_out, quad_in, top_out, top_in, down_out, down_in,
+    term_out, term_in, pair_out, pair_in, top_out, top_in, down_out, down_in,
     load_sem, ag_s, ag_r, halo_s, halo_r, rs_s, rs_r, relay_s, relay_r,
-    term_s, term_r, id_s, id_r, quad_s, quad_r, top_s, top_r, down_s, down_r,
+    term_s, term_r, id_s, id_r, pair_s, pair_r, top_s, top_r, down_s, down_r,
 ):
     me = lax.axis_index("clus")
     row = lax.axis_index("rhs")
     right = lax.rem(row + 1, RHS)
     left = lax.rem(row + RHS - 1, RHS)
     opposite = lax.rem(row + 2, RHS)
-    corner = lax.rem(me, 4)
+    sibling = me + 1 - 2 * lax.rem(me, 2)
     above = lax.rem(me + 1, CLUS)
     below = lax.rem(me + CLUS - 1, CLUS)
 
@@ -65,7 +68,7 @@
     loads = [
         pltpu.make_async_copy(vec_h, vec, load_sem.at[0]),
         pltpu.make_async_copy(basis_h, basis, load_sem.at[1]),
-        pltpu.make_async_copy(tr_h, tr, load_sem.at[2]),
+        pltpu.make_async_copy(transfer_h, transfer, load_sem.at[2]),
         pltpu.make_async_copy(coup_h, coup, load_sem.at[3]),
     ]
     for k in range(4):
@@ -83,11 +86,54 @@
     diagonal = group_row == group_lane
     zero = jnp.zeros((COLS, LANES), F32)
 
+    padded[...] = jnp.zeros((FAR, LANES), jnp.int32)
+    padded[:, 0:LEAVES] = device_v[...] * LEAVES + leaf_v[...]
+    rows8 = lax.broadcasted_iota(jnp.int32, (FAR, LANES), 0)
+    codes_row = jnp.where(rows8 == 0, padded[...], 0)
+    for p in range(1, FAR):
+        codes_row += jnp.where(rows8 == p, pltpu.roll(padded[...], LEAVES * p, 1), 0)
+    codes_row = jnp.sum(codes_row, axis=0, keepdims=True)
+    codes[me] = codes_row
+
+    at = lax.broadcasted_iota(jnp.int32, (CLUS, LANES), 1)
+    down_at = lax.broadcasted_iota(jnp.int32, (CLUS, LANES), 0)
+
+    def earlier(mask):
+        ones = jnp.where(mask, 1, 0)
+        total = ones
+        for k in (1, 2, 4, 8, 16, 32, 64):
+            total = total + jnp.where(at >= k, pltpu.roll(total, k, 1), 0)
+        return total - ones
+
+    mine = (codes_row >> 4) == down_at
+    rank = earlier(mine)
+    partner = at >> 4
+    table = jnp.zeros((CLUS, LANES), jnp.int32)
+    for slot in range(SLOTS):
+        tile = (at & 15) * FAR + (partner >> 2) * 4 + ((slot - partner) & 3)
+        tile = jnp.where(mine & (rank == slot), tile - EMPTY, 0)
+        table = jnp.where(at == slot, EMPTY + jnp.sum(tile, axis=1, keepdims=True), table)
+    source_v[...] = table
+    table_copy = pltpu.make_async_copy(source_v, source_s, load_sem.at[9])
+    table_copy.start()
+
+    loads[2].wait()
+    spot = lax.broadcasted_iota(jnp.int32, (RANK, LANES), 1)
+    same = (spot & (RANK - 1)) == lax.broadcasted_iota(jnp.int32, (RANK, LANES), 0)
+    wide = dot_nn(transfer[...], jnp.where(same, 1.0, 0.0).astype(BF16))
+    chip_place = lax.rem(me // 2, 2) * 2
+    for i in range(LEAVES):
+        place = chip_place + (parent_s[i] & 1)
+        tr[i * RANK : (i + 1) * RANK, :] = jnp.where(
+            (spot >> 5) == place, wide[i * RANK : (i + 1) * RANK], 0.0
+        ).astype(BF16)
+
     loads[0].wait()
     for i in range(LEAVES):
         win0[row, LEAVES + i] = vec[:, i * LEAF : (i + 1) * LEAF]
     loads[1].wait()
-    loads[2].wait()
+    loads[3].wait()
+    table_copy.wait()
 
     pending = []
 
@@ -115,11 +161,6 @@
 
     for q in range(2):
         win = (win0, win1)[q]
-        if q == 0:
-            pl.semaphore_wait(barrier, CLUS - 1 + RHS - 1)
-            for chunk in ORDER:
-                own_chunk(0, chunk)
-
         coeffs = []
         top_sum = zero
         for g in range(GROUPS):
@@ -133,18 +174,12 @@
             for t in range(1, GROUPS):
                 joined = joined + product[t * COLS : (t + 1) * COLS]
             top_sum = top_sum + dot_nn(joined.astype(BF16), tr[g * LANES : (g + 1) * LANES, :])
-        quad_out[q] = top_sum
-        quads = []
-        for o in range(1, 4):
-            peer = me - corner + lax.rem(corner + o, 4)
-            copy = send(quad_out.at[q], quad_in.at[q, o - 1],
-                        quad_s.at[q, o - 1], quad_r.at[q, o - 1], (peer, row))
-            copy.start()
-            quads.append(copy)
-        pending += quads
-
-        if q == 0:
-            loads[3].wait()
+        pair_out[q] = top_sum
+        pair = send(pair_out.at[q], pair_in.at[q], pair_s.at[q], pair_r.at[q], (sibling, row))
+        pending.append(pair)
+        if q == 1:
+            pair.start()
+
         for g in range(GROUPS):
             terms = dot_nn(coeffs[g], coup[g * LANES : (g + 1) * LANES, :])
             for t in range(GROUPS):
@@ -155,21 +190,14 @@
                     for k in range(1, 4):
                         rolled[base + k] = pltpu.roll(tile, RANK * k, 1)
 
-        for copy in quads:
-            copy.wait_recv()
-        top_tile = (top_sum + quad_in[q, 0] + quad_in[q, 1] + quad_in[q, 2]).astype(BF16)
-        top_out[q] = top_tile
-        top_in[q, me // 4] = top_tile
-
-        def top_start(o, c):
-            send(top_out.at[q], top_in.at[q, me // 4], top_s.at[q], top_r.at[q],
-                 (lax.rem(me + 4 * o, CLUS), row)).start()
-            return c
-
-        lax.fori_loop(1, CLUS // 4, top_start, 0)
+        if q == 0:
+            pl.semaphore_wait(barrier, CLUS - 1 + RHS - 1)
+            pair.start()
+            for chunk in ORDER:
+                own_chunk(0, chunk)
 
         def packed(d):
-            parts = [rolled[source_s[d * SLOTS + s]] for s in range(SLOTS)]
+            parts = [rolled[source_s[d, s]] for s in range(SLOTS)]
             low = jnp.where(lane == 0, parts[0], parts[1])
             high = jnp.where(lane == 2, parts[2], parts[3])
             return jnp.where(lane < 2, low, high).astype(BF16)
@@ -178,7 +206,7 @@
             return send(term_out.at[q, d], term_in.at[q, me], term_s.at[q], term_r.at[q], (d, row))
 
         def id_copy(d):
-            return send(ids_h.at[d], ids_in.at[me], id_s, id_r, (d, row))
+            return send(codes.at[me], codes.at[me], id_s, id_r, (d, row))
 
         def term_start(o, c):
             d = lax.rem(me + o, CLUS)
@@ -190,9 +218,18 @@
 
         lax.fori_loop(1, CLUS, term_start, 0)
         term_in[q, me] = packed(me)
-        if q == 0:
-            own_ids = pltpu.make_async_copy(ids_h.at[me], ids_in.at[me], load_sem.at[9])
-            own_ids.start()
+
+        pair.wait_recv()
+        top_tile = (top_sum + pair_in[q]).astype(BF16)
+        top_out[q] = top_tile
+        top_in[q, me // 2] = top_tile
+
+        def top_start(o, c):
+            send(top_out.at[q], top_in.at[q, me // 2], top_s.at[q], top_r.at[q],
+                 (lax.rem(me + 2 * o, CLUS), row)).start()
+            return c
+
+        lax.fori_loop(1, CLUS // 2, top_start, 0)
 
         halos = []
         for chunk in ORDER:
@@ -219,12 +256,12 @@
             for k in range(4):
                 loads[4 + k].wait()
         pltpu.make_async_copy(
-            top_in.at[q, pl.ds(0, CLUS // 4 - 1)], top_in.at[q, pl.ds(0, CLUS // 4 - 1)], top_r.at[q]
+            top_in.at[q, pl.ds(0, CLUS // 2 - 1)], top_in.at[q, pl.ds(0, CLUS // 2 - 1)], top_r.at[q]
         ).wait()
         pairs = CLUS // 4
         tops = [None] * pairs
         for m in range(pairs):
-            tops[(m + pairs // 2) % pairs] = top_in[q, m]
+            tops[(m + pairs // 2) % pairs] = top_in[q, 2 * m] + top_in[q, 2 * m + 1]
         local = dot_nt(jnp.concatenate(tops, axis=1), topc[...])
         down_out[q] = jnp.where(lane == lax.rem(me, 4), local, 0.0).astype(BF16)
         across = lax.rem(me + CLUS // 2, CLUS)
@@ -259,7 +296,7 @@
                 leaf = chunk * GROUPS + n
                 total = None
                 for p in range(2):
-                    j = near_s[leaf, p]
+                    j = near_s[p, leaf]
                     slot = lax.rem(j - me * LEAVES + LEAVES + CLUS * LEAVES, CLUS * LEAVES)
                     slot = jnp.minimum(slot, 3 * LEAVES - 1)
                     block = win[:, slot].reshape(RHS * COLS, LEAF)
@@ -291,16 +328,23 @@
             term_in.at[q, pl.ds(0, CLUS - 1)], term_in.at[q, pl.ds(0, CLUS - 1)], term_r.at[q]
         ).wait()
         if q == 0:
-            own_ids.wait()
             pltpu.make_async_copy(
-                ids_in.at[pl.ds(0, CLUS - 1)], ids_in.at[pl.ds(0, CLUS - 1)], id_r
+                codes.at[pl.ds(0, CLUS - 1)], codes.at[pl.ds(0, CLUS - 1)], id_r
             ).wait()
+            arrived = codes[...].reshape(CLUS, LANES)
+            mine = (arrived >> 4) == me
+            rank = earlier(mine)
+            table = jnp.zeros((CLUS, LANES), jnp.int32)
+            for slot in range(SLOTS):
+                target = jnp.where(mine & (rank == slot), (arrived & 15) + 1, 0)
+                table = jnp.where((at >> 5) == slot, jnp.sum(target, axis=1, keepdims=True), table)
+            ids[...] = table
 
         def add_terms(s, sums):
             values = term_in[q, s].astype(F32)
-            targets = ids_in[s].astype(F32)
+            targets = jnp.broadcast_to(ids[pl.ds(s, 1), :], (COLS, LANES))
             return tuple(
-                sums[t] + jnp.where(targets == float(t + 1), values, 0.0) for t in range(LEAVES)
+                sums[t] + jnp.where(targets == t + 1, values, 0.0) for t in range(LEAVES)
             )
 
         sums = lax.fori_loop(0, CLUS, add_terms, (zero,) * LEAVES)
@@ -339,45 +383,20 @@
         copy.wait_send()
     for q in range(2):
         pltpu.make_async_copy(
-            top_in.at[q, pl.ds(0, CLUS // 4 - 1)], top_in.at[q, pl.ds(0, CLUS // 4 - 1)], top_s.at[q]
+            top_in.at[q, pl.ds(0, CLUS // 2 - 1)], top_in.at[q, pl.ds(0, CLUS // 2 - 1)], top_s.at[q]
         ).wait()
         pltpu.make_async_copy(
             term_in.at[q, pl.ds(0, CLUS - 1)], term_in.at[q, pl.ds(0, CLUS - 1)], term_s.at[q]
         ).wait()
     pltpu.make_async_copy(
-        ids_in.at[pl.ds(0, CLUS - 1)], ids_in.at[pl.ds(0, CLUS - 1)], id_s
+        codes.at[pl.ds(0, CLUS - 1)], codes.at[pl.ds(0, CLUS - 1)], id_s
     ).wait()
-
-
-def slot_tables(far_device, far_leaf):
-    target = far_device.reshape(-1)
-    count = target.shape[0]
-    order = jnp.arange(count, dtype=jnp.int32)
-    same = target[:, None] == target[None, :]
-    rank = jnp.sum((same & (order[None, :] < order[:, None])).astype(jnp.int32), axis=1)
-    partner = order % FAR
-    code = (order // FAR) * FAR + (partner // 4) * 4 + (rank - partner + FAR) % 4
-    slot = target * SLOTS + rank
-    hit = slot[None, :] == jnp.arange(CLUS * SLOTS, dtype=jnp.int32)[:, None]
-    source = EMPTY + jnp.sum(jnp.where(hit, code[None, :] - EMPTY, 0), axis=1)
-    leaf = jnp.sum(jnp.where(hit, far_leaf.reshape(-1)[None, :] + 1, 0), axis=1)
-    tile = jnp.broadcast_to(
-        leaf.astype(BF16).reshape(CLUS, 1, SLOTS, 1), (CLUS, COLS, SLOTS, RANK)
-    ).reshape(CLUS, COLS, LANES)
-    return source.astype(jnp.int32), tile
 
 
 def on_device(
     vectors, near_field_tiles, near_lists, leaf_basis_set, far_coupling,
     far_device, far_leaf, transfer, parent, top_coupling,
 ):
-    source, ids = slot_tables(far_device, far_leaf)
-    chip = lax.axis_index("clus") // 2
-    place = (chip % 2) * 2 + parent % 2
-    hot = place[:, None, None, None] == jnp.arange(4, dtype=jnp.int32)[None, None, :, None]
-    tr = jnp.where(hot, transfer[:, :, None, :], jnp.zeros((), BF16)).reshape(
-        LEAVES * RANK, LANES
-    )
     vmem = lambda shape, dtype=BF16: pltpu.VMEM(shape, dtype)
     dma = lambda *shape: pltpu.SemaphoreType.DMA(shape)
     anywhere = pl.BlockSpec(memory_space=pltpu.HBM)
@@ -386,16 +405,21 @@
     return pl.pallas_call(
         kernel,
         out_shape=[jax.ShapeDtypeStruct(vectors.shape, BF16)] * 2,
-        in_specs=[smem, smem] + [anywhere] * 7,
+        in_specs=[smem, smem, whole, whole] + [anywhere] * 6,
         out_specs=[whole] * 2,
         scratch_shapes=[
             vmem((COLS, LEAVES * LEAF)),
             vmem((LEAVES, 2, LEAF, LEAF)),
             vmem((LEAVES * RANK, LEAF)),
             vmem((LEAVES * RANK, FAR * RANK)),
+            vmem((LEAVES * RANK, RANK)),
             vmem((LEAVES * RANK, LANES)),
             vmem((4 * RANK, CLUS * RANK)),
-            vmem((CLUS, COLS, LANES)),
+            vmem((CLUS, 1, LANES), jnp.int32),
+            vmem((FAR, LANES), jnp.int32),
+            vmem((CLUS, LANES), jnp.int32),
+            pltpu.SMEM((CLUS, LANES), jnp.int32),
+            vmem((CLUS, LANES), jnp.int32),
             vmem((RHS, 3 * LEAVES, COLS, LEAF)),
             vmem((RHS, 3 * LEAVES, COLS, LEAF)),
             vmem((2, RHS, LEAVES, COLS, LEAF)),
@@ -406,9 +430,9 @@
             vmem((2, CLUS, COLS, LANES)),
             vmem((2, CLUS, COLS, LANES)),
             vmem((2, COLS, LANES), F32),
-            vmem((2, 3, COLS, LANES), F32),
+            vmem((2, COLS, LANES), F32),
             vmem((2, COLS, LANES)),
-            vmem((2, CLUS // 4, COLS, LANES)),
+            vmem((2, CLUS // 2, COLS, LANES)),
             vmem((2, COLS, LANES)),
             vmem((2, 2, COLS, LANES)),
             dma(10),
@@ -418,19 +442,19 @@
             dma(2, GROUPS), dma(2, GROUPS),
             dma(2), dma(2),
             pltpu.SemaphoreType.DMA, pltpu.SemaphoreType.DMA,
-            dma(2, 3), dma(2, 3),
+            dma(2), dma(2),
             dma(2), dma(2),
             dma(2, 2), dma(2, 2),
         ],
         compiler_params=pltpu.CompilerParams(
-            collective_id=0, has_side_effects=True, vmem_limit_bytes=40 * 1024 * 1024
+            collective_id=0, has_side_effects=True, vmem_limit_bytes=VM * 1024 * 1024
         ),
     )(
-        near_lists, source,
+        near_lists.T, parent, far_device.T, far_leaf.T,
         vectors, near_field_tiles,
         leaf_basis_set.reshape(LEAVES * RANK, LEAF),
         far_coupling.reshape(LEAVES * RANK, FAR * RANK),
-        tr, top_coupling, ids,
+        transfer.reshape(LEAVES * RANK, RANK), top_coupling,
     )
 
 

time: 83.2 us -> 70 us (0.84)
  local copies, waits for them, and re-layouts: 9.6 us -> 3.14 us
  Pallas kernels: 69.1 us -> 66 us
  other arithmetic: 3 us -> 0 us
    unnamed x14 -> x2, local copies, waits for them, and re-layouts: 8.72 us -> 3.14 us
    pallas_call x1, Pallas kernels: 69.1 us -> 66 us  [on_device(): pl.pallas_call(kernel, out_shape=[jax.ShapeDtypeStruct(vectors.shape, BF1...]
    add x3 -> x0, other arithmetic: 1.36 us -> none  [the longest x1 0.69 us: slot_tables(): leaf = jnp.sum(jnp.where(hit, far_leaf.reshape(-1)[None, :] + 1, 0), axis=1)]
    select_n x1 -> x0, other arithmetic: 1.21 us -> none  [on_device(): jnp.where(hot, transfer[:, :, None, :], jnp.zeros((), BF16))]
where the time goes in v4:
time: 70 us; the launch traced here: 69.8 us
  Pallas kernels  66 us (94%)
  local copies, waits for them, and re-layouts  3.14 us (4%)
    pallas_call x1, Pallas kernels, on_device(): pl.pallas_call(kernel, out_shape=[jax.ShapeDtypeStruct(vectors.shape, BF1...  66 us
    unnamed x2, local copies, waits for them, and re-layouts  3.14 us

profile of v4, /device:TPU:2, one launch (start us, length us, event | category | flops | bytes accessed | tf_op | source)
XLA Modules:
  0.0 69.8 jit_solution(2899249074026528737)
XLA Ops:
  0.6 66.0 %shard_map.113 = (bf16[16,4096]{1,0:T(8,128)(2,1)}, bf16[16,4096]{1,0:T(8,128)(2,1)}) custom-call(s32[2,16]{1,0:T(2,128)} %bitcast.11, s32[16]{0:T(128)} %parent_s.1, s32[8,16]{1,0:T(8,128)} %bitcast.9, s32[8,16]{1,0:T(8,128)} %bitcast.10, bf16[16,4096]{1,0:T(8,128)(2,1)} %vec_h.1, bf16[16,2,256,256]{3,2,1,0:T(8,128)(2,1)} %tiles_h.1, ...), custom_call_target="tpu_custom_call" | custom-call | tf_op jit(solution)/shard_map/pallas_call | solution.py:405
  66.7 1.6 %copy.14 = bf16[16,4096]{1,0:T(8,128)(2,1)} copy(bf16[16,4096]{1,0:T(8,128)(2,1)} %get-tuple-element.4) | data formatting | bytes 262144
  68.2 1.6 %copy.15 = bf16[16,4096]{1,0:T(8,128)(2,1)} copy(bf16[16,4096]{1,0:T(8,128)(2,1)} %get-tuple-element.5) | data formatting | bytes 262144

commit v5 on v4

--- a/solution.py
+++ b/solution.py
@@ -31,7 +31,7 @@
     near_s, parent_s, device_v, leaf_v,
     vec_h, tiles_h, basis_h, coup_h, transfer_h, topc_h,
     out1, out2,
-    vec, tiles, basis, coup, transfer, tr, topc, codes, padded, source_v, source_s, ids,
+    vec, tiles, basis, coup, transfer, tr, own_topc, codes, padded, source_v, source_s, ids,
     win0, win1, part, rs, relay, rolled, far,
     term_out, term_in, pair_out, pair_in, top_out, top_in, down_out, down_in,
     load_sem, ag_s, ag_r, halo_s, halo_r, rs_s, rs_r, relay_s, relay_r,
@@ -71,11 +71,9 @@
         pltpu.make_async_copy(transfer_h, transfer, load_sem.at[2]),
         pltpu.make_async_copy(coup_h, coup, load_sem.at[3]),
     ]
+    loads.append(pltpu.make_async_copy(tiles_h, tiles, load_sem.at[4]))
     for k in range(4):
-        loads.append(
-            pltpu.make_async_copy(topc_h, topc.at[pl.ds(k * RANK, RANK)], load_sem.at[4 + k])
-        )
-    loads.append(pltpu.make_async_copy(tiles_h, tiles, load_sem.at[8]))
+        loads.append(pltpu.make_async_copy(topc_h, own_topc.at[k], load_sem.at[6 + k]))
     for copy in loads:
         copy.start()
     rolled[EMPTY] = jnp.zeros((COLS, LANES), F32)
@@ -114,7 +112,7 @@
         tile = jnp.where(mine & (rank == slot), tile - EMPTY, 0)
         table = jnp.where(at == slot, EMPTY + jnp.sum(tile, axis=1, keepdims=True), table)
     source_v[...] = table
-    table_copy = pltpu.make_async_copy(source_v, source_s, load_sem.at[9])
+    table_copy = pltpu.make_async_copy(source_v, source_s, load_sem.at[5])
     table_copy.start()
 
     loads[2].wait()
@@ -135,6 +133,7 @@
     loads[3].wait()
     table_copy.wait()
 
+    across = lax.rem(me + CLUS // 2, CLUS)
     pending = []
 
     def own_chunk(q, chunk):
@@ -196,6 +195,18 @@
             for chunk in ORDER:
                 own_chunk(0, chunk)
 
+        pair.wait_recv()
+        top_tile = (top_sum + pair_in[q]).astype(BF16)
+        top_out[q] = top_tile
+        top_in[q, me // 2] = top_tile
+
+        def top_start(o, c):
+            send(top_out.at[q], top_in.at[q, me // 2], top_s.at[q], top_r.at[q],
+                 (lax.rem(me + 2 * o, CLUS), row)).start()
+            return c
+
+        lax.fori_loop(1, CLUS // 2, top_start, 0)
+
         def packed(d):
             parts = [rolled[source_s[d, s]] for s in range(SLOTS)]
             low = jnp.where(lane == 0, parts[0], parts[1])
@@ -210,26 +221,17 @@
 
         def term_start(o, c):
             d = lax.rem(me + o, CLUS)
-            term_out[q, d] = packed(d)
             term_copy(d).start()
             if q == 0:
                 id_copy(d).start()
             return c
 
-        lax.fori_loop(1, CLUS, term_start, 0)
-        term_in[q, me] = packed(me)
-
-        pair.wait_recv()
-        top_tile = (top_sum + pair_in[q]).astype(BF16)
-        top_out[q] = top_tile
-        top_in[q, me // 2] = top_tile
-
-        def top_start(o, c):
-            send(top_out.at[q], top_in.at[q, me // 2], top_s.at[q], top_r.at[q],
-                 (lax.rem(me + 2 * o, CLUS), row)).start()
+        def pack(d, c):
+            term_out[q, d] = packed(d)
             return c
 
-        lax.fori_loop(1, CLUS // 2, top_start, 0)
+        lax.fori_loop(0, CLUS, pack, 0)
+        term_in[q, me] = term_out[q, me]
 
         halos = []
         for chunk in ORDER:
@@ -252,32 +254,42 @@
                 copy.start()
             pending += more
 
-        if q == 0:
-            for k in range(4):
-                loads[4 + k].wait()
-        pltpu.make_async_copy(
-            top_in.at[q, pl.ds(0, CLUS // 2 - 1)], top_in.at[q, pl.ds(0, CLUS // 2 - 1)], top_r.at[q]
-        ).wait()
-        pairs = CLUS // 4
-        tops = [None] * pairs
-        for m in range(pairs):
-            tops[(m + pairs // 2) % pairs] = top_in[q, 2 * m] + top_in[q, 2 * m + 1]
-        local = dot_nt(jnp.concatenate(tops, axis=1), topc[...])
-        down_out[q] = jnp.where(lane == lax.rem(me, 4), local, 0.0).astype(BF16)
-        across = lax.rem(me + CLUS // 2, CLUS)
-        for k, d in enumerate((across, across + 1 - 2 * lax.rem(across, 2))):
-            copy = send(down_out.at[q], down_in.at[q, k],
-                        down_s.at[q, k], down_r.at[q, k], (d, row))
-            copy.start()
-            pending.append(copy)
-        downs = pending[-2:]
+        def top_level(rows):
+            pltpu.make_async_copy(
+                top_in.at[q, pl.ds(0, CLUS // 2 - 1)], top_in.at[q, pl.ds(0, CLUS // 2 - 1)], top_r.at[q]
+            ).wait()
+            pairs = CLUS // 4
+            tops = [None] * pairs
+            for m in range(pairs):
+                tops[(m + pairs // 2) % pairs] = top_in[q, 2 * m] + top_in[q, 2 * m + 1]
+            return dot_nt(
+                jnp.concatenate(tops, axis=1), rows[...].reshape(4 * RANK, CLUS * RANK)
+            )
+
+        downs = []
+
+        def owner_block():
+            if q == 0:
+                for copy in loads[5:]:
+                    copy.wait()
+            local = top_level(own_topc)
+            down_out[q] = jnp.where(lane == lax.rem(me, 4), local, 0.0).astype(BF16)
+            for k, d in enumerate((across, across + 1 - 2 * lax.rem(across, 2))):
+                copy = send(down_out.at[q], down_in.at[q, k], down_s.at[q, k], down_r.at[q, k],
+                            (d, row))
+                copy.start()
+                downs.append(copy)
+            pending.extend(downs)
+
+        owner_block()
+        lax.fori_loop(1, CLUS, term_start, 0)
 
         for chunk in ORDER:
             for o, source in ((0, row), (1, left), (3, right), (2, opposite)):
                 for copy in spread(q, o, source, chunk):
                     copy.wait_recv()
         if q == 0:
-            loads[8].wait()
+            loads[4].wait()
 
         def relay_copy(chunk):
             leaves = pl.ds(chunk * GROUPS, GROUPS)
@@ -414,7 +426,7 @@
             vmem((LEAVES * RANK, FAR * RANK)),
             vmem((LEAVES * RANK, RANK)),
             vmem((LEAVES * RANK, LANES)),
-            vmem((4 * RANK, CLUS * RANK)),
+            vmem((4, RANK, CLUS * RANK)),
             vmem((CLUS, 1, LANES), jnp.int32),
             vmem((FAR, LANES), jnp.int32),
             vmem((CLUS, LANES), jnp.int32),

time: 70 us -> 63.1 us (0.901)
  Pallas kernels: 66 us -> 59.1 us
    pallas_call x1, Pallas kernels: 66 us -> 59.1 us  [on_device(): pl.pallas_call(kernel, out_shape=[jax.ShapeDtypeStruct(vectors.shape, BF1...]
where the time goes in v5:
time: 63.1 us; the launch traced here: 62.9 us
  Pallas kernels  59.1 us (94%)
  local copies, waits for them, and re-layouts  3.14 us (5%)
  between operations  0.64 us (1%)
    pallas_call x1, Pallas kernels, on_device(): pl.pallas_call(kernel, out_shape=[jax.ShapeDtypeStruct(vectors.shape, BF1...  59.1 us
    unnamed x2, local copies, waits for them, and re-layouts  3.14 us

profile of v5, /device:TPU:2, one launch (start us, length us, event | category | flops | bytes accessed | tf_op | source)
XLA Modules:
  0.0 62.9 jit_solution(12049560792879479423)
XLA Ops:
  0.6 59.1 %shard_map.113 = (bf16[16,4096]{1,0:T(8,128)(2,1)}, bf16[16,4096]{1,0:T(8,128)(2,1)}) custom-call(s32[2,16]{1,0:T(2,128)} %bitcast.11, s32[16]{0:T(128)} %parent_s.1, s32[8,16]{1,0:T(8,128)} %bitcast.9, s32[8,16]{1,0:T(8,128)} %bitcast.10, bf16[16,4096]{1,0:T(8,128)(2,1)} %vec_h.1, bf16[16,2,256,256]{3,2,1,0:T(8,128)(2,1)} %tiles_h.1, ...), custom_call_target="tpu_custom_call" | custom-call | tf_op jit(solution)/shard_map/pallas_call | solution.py:417
  59.7 1.6 %copy.14 = bf16[16,4096]{1,0:T(8,128)(2,1)} copy(bf16[16,4096]{1,0:T(8,128)(2,1)} %get-tuple-element.4) | data formatting | bytes 262144
  61.3 1.6 %copy.15 = bf16[16,4096]{1,0:T(8,128)(2,1)} copy(bf16[16,4096]{1,0:T(8,128)(2,1)} %get-tuple-element.5) | data formatting | bytes 262144

commit v6 on v5

--- a/solution.py
+++ b/solution.py
@@ -200,12 +200,17 @@
         top_out[q] = top_tile
         top_in[q, me // 2] = top_tile
 
-        def top_start(o, c):
-            send(top_out.at[q], top_in.at[q, me // 2], top_s.at[q], top_r.at[q],
-                 (lax.rem(me + 2 * o, CLUS), row)).start()
+        def top_send(d):
+            send(top_out.at[q], top_in.at[q, me // 2], top_s.at[q], top_r.at[q], (d, row)).start()
+
+        def top_start(j, c):
+            k = 2 * j
+            top_send(lax.rem(me + k, CLUS))
+            top_send(lax.rem(me + CLUS - k, CLUS))
             return c
 
-        lax.fori_loop(1, CLUS // 2, top_start, 0)
+        lax.fori_loop(1, CLUS // 4, top_start, 0)
+        top_send(across)
 
         def packed(d):
             parts = [rolled[source_s[d, s]] for s in range(SLOTS)]
@@ -213,18 +218,12 @@
             high = jnp.where(lane == 2, parts[2], parts[3])
             return jnp.where(lane < 2, low, high).astype(BF16)
 
-        def term_copy(d):
-            return send(term_out.at[q, d], term_in.at[q, me], term_s.at[q], term_r.at[q], (d, row))
+        def term_copy(d, g):
+            return send(term_out.at[q, d], term_in.at[q, me], term_s.at[q], term_r.at[q, g],
+                        (d, row))
 
         def id_copy(d):
             return send(codes.at[me], codes.at[me], id_s, id_r, (d, row))
-
-        def term_start(o, c):
-            d = lax.rem(me + o, CLUS)
-            term_copy(d).start()
-            if q == 0:
-                id_copy(d).start()
-            return c
 
         def pack(d, c):
             term_out[q, d] = packed(d)
@@ -282,7 +281,27 @@
             pending.extend(downs)
 
         owner_block()
-        lax.fori_loop(1, CLUS, term_start, 0)
+        def away(g, j):
+            return 8 * g + 1 + j
+
+        def distances(g):
+            return 0, (7 if g == GROUPS - 1 else 8)
+
+        single = GROUPS - 1
+        for g in range(GROUPS):
+            def term_start(j, c):
+                k = away(g, j)
+                for d in (lax.rem(me + k, CLUS), lax.rem(me + CLUS - k, CLUS)):
+                    term_copy(d, g).start()
+                    if q == 0:
+                        id_copy(d).start()
+                return c
+
+            if g == single:
+                term_copy(across, g).start()
+                if q == 0:
+                    id_copy(across).start()
+            lax.fori_loop(*distances(g), term_start, 0)
 
         for chunk in ORDER:
             for o, source in ((0, row), (1, left), (3, right), (2, opposite)):
@@ -336,9 +355,6 @@
             copy.start()
             pending.append(copy)
 
-        pltpu.make_async_copy(
-            term_in.at[q, pl.ds(0, CLUS - 1)], term_in.at[q, pl.ds(0, CLUS - 1)], term_r.at[q]
-        ).wait()
         if q == 0:
             pltpu.make_async_copy(
                 codes.at[pl.ds(0, CLUS - 1)], codes.at[pl.ds(0, CLUS - 1)], id_r
@@ -359,7 +375,21 @@
                 sums[t] + jnp.where(targets == t + 1, values, 0.0) for t in range(LEAVES)
             )
 
-        sums = lax.fori_loop(0, CLUS, add_terms, (zero,) * LEAVES)
+        sums = add_terms(me, (zero,) * LEAVES)
+        for g in range(GROUPS):
+            def add_both(j, sums):
+                k = away(g, j)
+                sums = add_terms(lax.rem(me + k, CLUS), sums)
+                return add_terms(lax.rem(me + CLUS - k, CLUS), sums)
+
+            low, high = distances(g)
+            count = 2 * (high - low) + (1 if g == single else 0)
+            pltpu.make_async_copy(
+                term_in.at[q, pl.ds(0, count)], term_in.at[q, pl.ds(0, count)], term_r.at[q, g]
+            ).wait()
+            if g == single:
+                sums = add_terms(across, sums)
+            sums = lax.fori_loop(low, high, add_both, sums)
 
         for copy in downs:
             copy.wait_recv()
@@ -452,7 +482,7 @@
             dma(2, 2, RHS, GROUPS), dma(2, 2, RHS, GROUPS),
             dma(2, 2, GROUPS), dma(2, 2, GROUPS),
             dma(2, GROUPS), dma(2, GROUPS),
-            dma(2), dma(2),
+            dma(2), dma(2, GROUPS),
             pltpu.SemaphoreType.DMA, pltpu.SemaphoreType.DMA,
             dma(2), dma(2),
             dma(2), dma(2),

time: 63.1 us -> 62.6 us (level)
  no operation moved by 1% of the time
where the time goes in v6:
time: 62.6 us; the launch traced here: 62.4 us
  Pallas kernels  58.6 us (94%)
  local copies, waits for them, and re-layouts  3.14 us (5%)
  between operations  0.64 us (1%)
    pallas_call x1, Pallas kernels, on_device(): pl.pallas_call(kernel, out_shape=[jax.ShapeDtypeStruct(vectors.shape, BF1...  58.6 us
    unnamed x2, local copies, waits for them, and re-layouts  3.14 us

profile of v6, /device:TPU:2, one launch (start us, length us, event | category | flops | bytes accessed | tf_op | source)
XLA Modules:
  0.0 62.4 jit_solution(8158458580028077688)
XLA Ops:
  0.6 58.6 %shard_map.113 = (bf16[16,4096]{1,0:T(8,128)(2,1)}, bf16[16,4096]{1,0:T(8,128)(2,1)}) custom-call(s32[2,16]{1,0:T(2,128)} %bitcast.11, s32[16]{0:T(128)} %parent_s.1, s32[8,16]{1,0:T(8,128)} %bitcast.9, s32[8,16]{1,0:T(8,128)} %bitcast.10, bf16[16,4096]{1,0:T(8,128)(2,1)} %vec_h.1, bf16[16,2,256,256]{3,2,1,0:T(8,128)(2,1)} %tiles_h.1, ...), custom_call_target="tpu_custom_call" | custom-call | tf_op jit(solution)/shard_map/pallas_call | solution.py:447
  59.3 1.6 %copy.14 = bf16[16,4096]{1,0:T(8,128)(2,1)} copy(bf16[16,4096]{1,0:T(8,128)(2,1)} %get-tuple-element.4) | data formatting | bytes 262144
  60.8 1.6 %copy.15 = bf16[16,4096]{1,0:T(8,128)(2,1)} copy(bf16[16,4096]{1,0:T(8,128)(2,1)} %get-tuple-element.5) | data formatting | bytes 262144

commit v7 on v6

--- a/solution.py
+++ b/solution.py
@@ -30,7 +30,7 @@
 def kernel(
     near_s, parent_s, device_v, leaf_v,
     vec_h, tiles_h, basis_h, coup_h, transfer_h, topc_h,
-    out1, out2,
+    both,
     vec, tiles, basis, coup, transfer, tr, own_topc, codes, padded, source_v, source_s, ids,
     win0, win1, part, rs, relay, rolled, far,
     term_out, term_in, pair_out, pair_in, top_out, top_in, down_out, down_in,
@@ -406,7 +406,7 @@
             for t in range(GROUPS):
                 far[GROUPS * g + t] = result[t * COLS : (t + 1) * COLS]
 
-        out = out1 if q == 0 else out2
+        out = both.at[q]
         for chunk in ORDER:
             rs_copy(chunk, 1 - chunk // 2).wait_recv()
             rs_copy(chunk, chunk // 2).wait_recv()
@@ -444,11 +444,11 @@
     anywhere = pl.BlockSpec(memory_space=pltpu.HBM)
     smem = pl.BlockSpec(memory_space=pltpu.SMEM)
     whole = pl.BlockSpec(memory_space=pltpu.VMEM)
-    return pl.pallas_call(
+    both = pl.pallas_call(
         kernel,
-        out_shape=[jax.ShapeDtypeStruct(vectors.shape, BF16)] * 2,
+        out_shape=jax.ShapeDtypeStruct((2,) + vectors.shape, BF16),
         in_specs=[smem, smem, whole, whole] + [anywhere] * 6,
-        out_specs=[whole] * 2,
+        out_specs=whole,
         scratch_shapes=[
             vmem((COLS, LEAVES * LEAF)),
             vmem((LEAVES, 2, LEAF, LEAF)),
@@ -498,6 +498,7 @@
         far_coupling.reshape(LEAVES * RANK, FAR * RANK),
         transfer.reshape(LEAVES * RANK, RANK), top_coupling,
     )
+    return both[0], both[1]
 
 
 def solution(mesh):

time: 62.6 us -> 61.1 us (0.976)
  local copies, waits for them, and re-layouts: 3.14 us -> 1.68 us
    unnamed x2 -> x0, local copies, waits for them, and re-layouts: 3.14 us -> none
    squeeze x0 -> x1, local copies, waits for them, and re-layouts: none -> 1.68 us  [on_device(): return (both[0], both[1])]
where the time goes in v7:
time: 61.1 us; the launch traced here: 61 us
  Pallas kernels  58.6 us (96%)
  local copies, waits for them, and re-layouts  1.68 us (3%)
  between operations  0.64 us (1%)
    pallas_call x1, Pallas kernels, on_device(): pl.pallas_call(kernel, out_shape=jax.ShapeDtypeStruct((2,) + vectors.shap...  58.6 us
    squeeze x1, local copies, waits for them, and re-layouts, on_device(): return (both[0], both[1])  1.68 us

profile of v7, /device:TPU:2, one launch (start us, length us, event | category | flops | bytes accessed | tf_op | source)
XLA Modules:
  0.0 61.0 jit_solution(16166798191066760537)
XLA Ops:
  0.6 58.6 %shard_map.113 = bf16[2,16,4096]{2,1,0:T(8,128)(2,1)} custom-call(s32[2,16]{1,0:T(2,128)} %bitcast.15, s32[16]{0:T(128)} %parent_s.1, s32[8,16]{1,0:T(8,128)} %bitcast.13, s32[8,16]{1,0:T(8,128)} %bitcast.14, bf16[16,4096]{1,0:T(8,128)(2,1)} %vec_h.1, bf16[16,2,256,256]{3,2,1,0:T(8,128)(2,1)} %tiles_h.1, bf16[512,256]{1,0:T(8,128)(2,1)} %bitcast.10, ...), custom_call_target="tpu_custom_call" | custom-call | tf_op jit(solution)/shard_map/pallas_call | solution.py:447
  59.3 1.7 %slice_bitcast_fusion = (bf16[16,4096]{1,0:T(8,128)(2,1)}, bf16[16,4096]{1,0:T(8,128)(2,1)}) fusion(bf16[2,16,4096]{2,1,0:T(8,128)(2,1)} %shard_map.113), kind=kLoop, calls=%fused_computation | loop fusion | bytes 524288 | tf_op jit(solution)/shard_map/squeeze | solution.py:501
